TPU v7x, 32 devices: a whole 2x2x4 slice. The times are simulated.
32 devices in a mesh: rep: 8 (over y, x, core), shard: 4 (over z).
Axes of the slice: x: 2, y: 2, z: 4, core: 2. Of those that a mesh axis runs over, the one named last changes fastest.
Arguments:
- tokens: bfloat16 [8192, 768], P(('rep', 'shard')), may hold values from -6 to 6
- cotangent: bfloat16 [8192, 768], P(('rep', 'shard')), may hold values from -6 to 6
- doc_ids: int32 [32, 256], P(('rep', 'shard')), may hold values from 0 to 3, never falling along the last dimension, each value on 1 to 192 neighbouring positions
- buckets: int32 [383], replicated, may hold values from 0 to 31
- routes: int32 [8192, 2], P(('rep', 'shard')), may hold values from 0 to 3, all different within a row; in each aligned block of 256 rows (0 to 255, 256 to 511, ...) at most 256 rows name the same one
- gain_attn: float32 [768], replicated, may hold values from 0.5 to 1.5
- gain_moe: float32 [768], replicated, may hold values from 0.5 to 1.5
- w_query: bfloat16 [768, 768], P('shard'), may hold values from -0.21875 to 0.21875
- w_key: bfloat16 [768, 768], P('shard'), may hold values from -0.21875 to 0.21875
- w_value: bfloat16 [768, 768], P('shard'), may hold values from -0.21875 to 0.21875
- w_proj: bfloat16 [768, 768], P('shard'), may hold values from -0.625 to 0.625
- rel_table: float32 [32, 12], replicated, may hold values from -3 to 3
- w_router: bfloat16 [768, 4], replicated, may hold values from -0.21875 to 0.21875
- w_in: bfloat16 [4, 768, 3072], P('shard'), may hold values from -0.21875 to 0.21875
- w_down: bfloat16 [4, 3072, 768], P('shard'), may hold values from -0.21875 to 0.21875
Outputs:
- mixed: bfloat16 [8192, 768], P(('rep', 'shard'))
- grad_tokens: float32 [8192, 768], P(('rep', 'shard'))
- grad_gain_attn: float32 [768], replicated
- grad_gain_moe: float32 [768], replicated
- grad_query: float32 [768, 768], P('shard')
- grad_key: float32 [768, 768], P('shard')
- grad_value: float32 [768, 768], P('shard')
- grad_proj: float32 [768, 768], P('shard')
- grad_table: float32 [32, 12], replicated
- grad_router: float32 [768, 4], replicated
- grad_in: float32 [4, 768, 3072], P('shard')
- grad_down: float32 [4, 3072, 768], P('shard')
Inputs may be any that keep to these rules, and one draw needn't show every extreme that they name: `routes`: each token names two different experts; among the 256 rows of one device no expert is named more than 256 times, and on some devices some expert is named exactly that often.
All inputs are finite; a program needn't handle non-finite values.
Results may differ from a plain program's by a relative error of at most 0.02.
Values may be sent and summed in bfloat16 or wider, within the bound.
A program may use at most 448 MiB of HBM per device.

v0:
```python
import jax
import jax.numpy as jnp
from jax import lax
from jax.sharding import PartitionSpec as P

HEADS = 12


EPS = 1e-06


def product(left, right):
    return jnp.dot(left, right, preferred_element_type=jnp.float32)


def inner_left(left, right):
    return lax.dot_general(
        left, right, (((0,), (0,)), ((), ())), preferred_element_type=jnp.float32
    )


def inner_right(left, right):
    return lax.dot_general(
        left, right, (((1,), (1,)), ((), ())), preferred_element_type=jnp.float32
    )


def rms_norm(features, gain_vec):
    return (
        features * lax.rsqrt(jnp.mean(features * features, axis=-1, keepdims=True) + EPS) * gain_vec
    )


def bucket_table(buckets, count):
    return (buckets[:, None] == jnp.arange(count, dtype=jnp.int32)[None, :]).astype(jnp.float32)


def position_bias(table_arg, buckets, rows_here):
    span = (buckets.shape[0] + 1) // 2
    steps_idx = jnp.arange(rows_here, dtype=jnp.int32)
    offset = jnp.clip(steps_idx[:, None] - steps_idx[None, :] + span - 1, 0, 2 * span - 2)
    per_gap = jnp.dot(
        bucket_table(buckets, table_arg.shape[0]), table_arg, precision=lax.Precision.HIGHEST
    )
    return jnp.transpose(jnp.take(per_gap, offset, axis=0), (2, 0, 1))


def table_gradient(grad_scores_low, buckets, table_rows):
    heads_here, rows_here, _ = grad_scores_low.shape
    span = (buckets.shape[0] + 1) // 2
    flipped = jnp.flip(grad_scores_low.astype(jnp.float32), axis=2)
    padded = jnp.pad(flipped, ((0, 0), (0, 0), (0, rows_here)))
    flat = padded.reshape(heads_here, rows_here * 2 * rows_here)[
        :, : rows_here * (2 * rows_here - 1)
    ]
    skewed = flat.reshape(heads_here, rows_here, 2 * rows_here - 1)
    diagonal_sums = jnp.sum(skewed, axis=1)
    kept = diagonal_sums[:, rows_here - span : rows_here + span - 1]
    return jnp.dot(bucket_table(buckets, table_rows).T, kept.T, precision=lax.Precision.HIGHEST)


def slot_layout(route_row, experts, capacity):
    flat_routes = route_row.reshape(-1)
    onehot = (flat_routes[:, None] == jnp.arange(experts, dtype=jnp.int32)[None, :]).astype(
        jnp.int32
    )
    before = jnp.cumsum(onehot, axis=0) - onehot
    slot_place = jnp.sum(before * onehot, axis=1)
    slot_index = flat_routes * capacity + slot_place
    source = jnp.arange(flat_routes.shape[0], dtype=jnp.int32) // 2
    slot_source = jnp.zeros((experts * capacity,), jnp.int32).at[slot_index].set(source)
    filled = jnp.zeros((experts * capacity,), jnp.float32).at[slot_index].set(1.0)
    return (slot_index.reshape(-1, 2), slot_source, filled)


def gate_values(logit_arg, route_row):
    expert_probs = jax.nn.softmax(logit_arg, axis=-1)
    picked = jnp.take_along_axis(expert_probs, route_row, axis=1)
    return picked / jnp.sum(picked, axis=1, keepdims=True)


def attention_scores(query_low, keys_low, pos_bias, same_doc):
    rows_here = query_low.shape[0]
    query_heads = query_low.reshape(rows_here, HEADS, -1)
    key_heads = keys_low.reshape(rows_here, HEADS, -1)
    scores = jnp.einsum(
        "ihd,jhd->hij", query_heads, key_heads, preferred_element_type=jnp.float32
    ) * query_heads.shape[2] ** (-0.5)
    return jnp.where(same_doc[None], scores + pos_bias, -1e30)


def expert_forward(slot_rows, w_first, w_second):
    hidden = jnp.einsum("ecd,edf->ecf", slot_rows, w_first, preferred_element_type=jnp.float32)
    act_low = jax.nn.gelu(hidden).astype(jnp.bfloat16)
    return jnp.einsum("ecf,efd->ecd", act_low, w_second, preferred_element_type=jnp.float32).astype(
        jnp.bfloat16
    )


def expert_backward(slot_rows, grad_out, w_first, w_second):
    hidden = jnp.einsum("ecd,edf->ecf", slot_rows, w_first, preferred_element_type=jnp.float32)
    act_full, gelu_pull = jax.vjp(jax.nn.gelu, hidden)
    act_low = act_full.astype(jnp.bfloat16)
    grad_act = jnp.einsum("ecd,efd->ecf", grad_out, w_second, preferred_element_type=jnp.float32)
    grad_hidden = gelu_pull(grad_act)[0].astype(jnp.bfloat16)
    grad_second = jnp.einsum("ecf,ecd->efd", act_low, grad_out, preferred_element_type=jnp.float32)
    grad_first = jnp.einsum(
        "ecd,ecf->edf", slot_rows, grad_hidden, preferred_element_type=jnp.float32
    )
    grad_rows = jnp.einsum(
        "ecf,edf->ecd", grad_hidden, w_first, preferred_element_type=jnp.float32
    ).astype(jnp.bfloat16)
    return (grad_rows, grad_first, grad_second)


def on_device(
    tokens,
    cotangent,
    doc_ids,
    buckets,
    routes,
    gain_attn,
    gain_moe,
    w_query,
    w_key,
    w_value,
    w_proj,
    rel_table,
    w_router,
    w_in,
    w_down,
):
    rows_here = tokens.shape[0]
    experts = w_router.shape[1]
    capacity = min(rows_here, 4 * rows_here // experts)
    inputs = tokens.astype(jnp.float32)
    doc_row = doc_ids[0]
    same_doc = doc_row[:, None] == doc_row[None, :]
    pos_bias = position_bias(rel_table, buckets, rows_here)
    h_first = rms_norm(inputs, gain_attn).astype(jnp.bfloat16)
    full_query, full_key, full_value, full_proj = (
        lax.all_gather(w_query, "shard", axis=0, tiled=True),
        lax.all_gather(w_key, "shard", axis=0, tiled=True),
        lax.all_gather(w_value, "shard", axis=0, tiled=True),
        lax.all_gather(w_proj, "shard", axis=0, tiled=True),
    )
    query_low = product(h_first, full_query).astype(jnp.bfloat16)
    keys_low = product(h_first, full_key).astype(jnp.bfloat16)
    values_low = product(h_first, full_value).astype(jnp.bfloat16)
    scores = attention_scores(query_low, keys_low, pos_bias, same_doc)
    row_peak = jnp.max(scores, axis=-1, keepdims=True)
    exp_total = jnp.sum(jnp.exp(scores - row_peak), axis=-1, keepdims=True)
    log_total = row_peak + jnp.log(exp_total)
    attn_probs = (jnp.exp(scores - row_peak) / exp_total).astype(jnp.bfloat16)
    value_heads = values_low.reshape(rows_here, HEADS, -1)
    mixed_heads = (
        jnp.einsum("hij,jhd->ihd", attn_probs, value_heads, preferred_element_type=jnp.float32)
        .reshape(rows_here, -1)
        .astype(jnp.bfloat16)
    )
    y_first = inputs + product(mixed_heads, full_proj)
    h_second = rms_norm(y_first, gain_moe).astype(jnp.bfloat16)
    logits = product(h_second, w_router)
    gates = gate_values(logits, routes)
    slot_index, slot_source, filled = slot_layout(routes, experts, capacity)
    flat_slots = slot_index.reshape(-1)
    slot_in = (h_second[slot_source] * filled[:, None].astype(jnp.bfloat16)).reshape(
        experts, capacity, -1
    )
    all_first, all_second = (
        lax.all_gather(w_in, "shard", axis=0, tiled=True),
        lax.all_gather(w_down, "shard", axis=0, tiled=True),
    )
    slot_out = expert_forward(slot_in, all_first, all_second)
    picked_rows = (
        slot_out.reshape(experts * capacity, -1)[flat_slots]
        .reshape(rows_here, 2, -1)
        .astype(jnp.float32)
    )
    mixed = (y_first + jnp.sum(gates[:, :, None] * picked_rows, axis=1)).astype(jnp.bfloat16)
    out_grad = cotangent.astype(jnp.float32)
    grad_gates = jnp.sum(out_grad[:, None, :] * picked_rows, axis=-1)
    gate_slot = jnp.zeros((experts * capacity,), jnp.float32).at[flat_slots].set(gates.reshape(-1))
    grad_slot = (
        (out_grad[slot_source] * gate_slot[:, None])
        .astype(jnp.bfloat16)
        .reshape(experts, capacity, -1)
    )
    again_first, again_second = (
        lax.all_gather(w_in, "shard", axis=0, tiled=True),
        lax.all_gather(w_down, "shard", axis=0, tiled=True),
    )
    grad_rows, whole_first, whole_second = expert_backward(
        slot_in, grad_slot, again_first, again_second
    )
    grad_h_second = jnp.sum(
        grad_rows.reshape(experts * capacity, -1)[flat_slots]
        .reshape(rows_here, 2, -1)
        .astype(jnp.float32),
        axis=1,
    )
    _, gate_pull = jax.vjp(lambda logit_arg: gate_values(logit_arg, routes), logits)
    grad_logits = gate_pull(grad_gates)[0]
    grad_router = jnp.dot(
        h_second.astype(jnp.float32).T, grad_logits, precision=lax.Precision.HIGHEST
    )
    grad_h_second = grad_h_second + jnp.dot(
        grad_logits, w_router.astype(jnp.float32).T, precision=lax.Precision.HIGHEST
    )
    _, second_pull = jax.vjp(rms_norm, y_first, gain_moe)
    grad_y_part, grad_gain_moe = second_pull(grad_h_second)
    grad_y_first = out_grad + grad_y_part
    grad_attn = grad_y_first.astype(jnp.bfloat16)
    back_query, back_key, back_value, back_proj = (
        lax.all_gather(w_query, "shard", axis=0, tiled=True),
        lax.all_gather(w_key, "shard", axis=0, tiled=True),
        lax.all_gather(w_value, "shard", axis=0, tiled=True),
        lax.all_gather(w_proj, "shard", axis=0, tiled=True),
    )
    grad_proj = inner_left(mixed_heads, grad_attn)
    grad_heads = (
        inner_right(grad_attn, back_proj).astype(jnp.bfloat16).reshape(rows_here, HEADS, -1)
    )
    scores_again = attention_scores(query_low, keys_low, pos_bias, same_doc)
    probs_full = jnp.exp(scores_again - log_total)
    probs_low = probs_full.astype(jnp.bfloat16)
    grad_probs = jnp.einsum(
        "ihd,jhd->hij", grad_heads, value_heads, preferred_element_type=jnp.float32
    )
    grad_values = (
        jnp.einsum("hij,ihd->jhd", probs_low, grad_heads, preferred_element_type=jnp.float32)
        .reshape(rows_here, -1)
        .astype(jnp.bfloat16)
    )
    grad_scores = probs_full * (
        grad_probs - jnp.sum(grad_probs * probs_full, axis=-1, keepdims=True)
    )
    grad_scores_low = grad_scores.astype(jnp.bfloat16)
    grad_table = table_gradient(grad_scores_low, buckets, rel_table.shape[0])
    query_heads = query_low.reshape(rows_here, HEADS, -1)
    key_heads = keys_low.reshape(rows_here, HEADS, -1)
    score_scale = query_heads.shape[2] ** (-0.5)
    grad_q = (
        (
            jnp.einsum(
                "hij,jhd->ihd", grad_scores_low, key_heads, preferred_element_type=jnp.float32
            )
            * score_scale
        )
        .reshape(rows_here, -1)
        .astype(jnp.bfloat16)
    )
    grad_k = (
        (
            jnp.einsum(
                "hij,ihd->jhd", grad_scores_low, query_heads, preferred_element_type=jnp.float32
            )
            * score_scale
        )
        .reshape(rows_here, -1)
        .astype(jnp.bfloat16)
    )
    grad_query = inner_left(h_first, grad_q)
    grad_key = inner_left(h_first, grad_k)
    grad_value = inner_left(h_first, grad_values)
    grad_h_first = (
        inner_right(grad_q, back_query)
        + inner_right(grad_k, back_key)
        + inner_right(grad_values, back_value)
    )
    _, first_pull = jax.vjp(rms_norm, inputs, gain_attn)
    grad_x_part, grad_gain_attn = first_pull(grad_h_first)
    grad_tokens = grad_y_first + grad_x_part
    own_query, own_key, own_value, own_proj, own_first, own_second = (
        lax.psum_scatter(
            grad_query.astype(jnp.bfloat16), "shard", scatter_dimension=0, tiled=True
        ).astype(jnp.float32),
        lax.psum_scatter(
            grad_key.astype(jnp.bfloat16), "shard", scatter_dimension=0, tiled=True
        ).astype(jnp.float32),
        lax.psum_scatter(
            grad_value.astype(jnp.bfloat16), "shard", scatter_dimension=0, tiled=True
        ).astype(jnp.float32),
        lax.psum_scatter(
            grad_proj.astype(jnp.bfloat16), "shard", scatter_dimension=0, tiled=True
        ).astype(jnp.float32),
        lax.psum_scatter(
            whole_first.astype(jnp.bfloat16), "shard", scatter_dimension=0, tiled=True
        ).astype(jnp.float32),
        lax.psum_scatter(
            whole_second.astype(jnp.bfloat16), "shard", scatter_dimension=0, tiled=True
        ).astype(jnp.float32),
    )
    part_query, part_key, part_value, part_proj, part_first, part_second = (
        lax.psum_scatter(
            own_query.astype(jnp.bfloat16), "rep", scatter_dimension=1, tiled=True
        ).astype(jnp.float32),
        lax.psum_scatter(
            own_key.astype(jnp.bfloat16), "rep", scatter_dimension=1, tiled=True
        ).astype(jnp.float32),
        lax.psum_scatter(
            own_value.astype(jnp.bfloat16), "rep", scatter_dimension=1, tiled=True
        ).astype(jnp.float32),
        lax.psum_scatter(
            own_proj.astype(jnp.bfloat16), "rep", scatter_dimension=1, tiled=True
        ).astype(jnp.float32),
        lax.psum_scatter(
            own_first.astype(jnp.bfloat16), "rep", scatter_dimension=1, tiled=True
        ).astype(jnp.float32),
        lax.psum_scatter(
            own_second.astype(jnp.bfloat16), "rep", scatter_dimension=1, tiled=True
        ).astype(jnp.float32),
    )
    sum_query, sum_key, sum_value, sum_proj, sum_first, sum_second = (
        lax.all_gather(part_query.astype(jnp.bfloat16), "rep", axis=1, tiled=True).astype(
            part_query.dtype
        ),
        lax.all_gather(part_key.astype(jnp.bfloat16), "rep", axis=1, tiled=True).astype(
            part_key.dtype
        ),
        lax.all_gather(part_value.astype(jnp.bfloat16), "rep", axis=1, tiled=True).astype(
            part_value.dtype
        ),
        lax.all_gather(part_proj.astype(jnp.bfloat16), "rep", axis=1, tiled=True).astype(
            part_proj.dtype
        ),
        lax.all_gather(part_first.astype(jnp.bfloat16), "rep", axis=1, tiled=True).astype(
            part_first.dtype
        ),
        lax.all_gather(part_second.astype(jnp.bfloat16), "rep", axis=1, tiled=True).astype(
            part_second.dtype
        ),
    )
    sum_gain_attn, sum_gain_moe, sum_table, sum_router = lax.psum(
        (grad_gain_attn, grad_gain_moe, grad_table, grad_router), ("rep", "shard")
    )
    return (
        mixed,
        grad_tokens,
        sum_gain_attn,
        sum_gain_moe,
        sum_query,
        sum_key,
        sum_value,
        sum_proj,
        sum_table,
        sum_router,
        sum_first,
        sum_second,
    )


def solution(mesh):
    in_specs = (
        P(("rep", "shard"), None),
        P(("rep", "shard"), None),
        P(("rep", "shard"), None),
        P(),
        P(("rep", "shard"), None),
        P(),
        P(),
        P("shard", None),
        P("shard", None),
        P("shard", None),
        P("shard", None),
        P(),
        P(),
        P("shard", None, None),
        P("shard", None, None),
    )
    out_specs = (
        P(("rep", "shard"), None),
        P(("rep", "shard"), None),
        P(),
        P(),
        P("shard", None),
        P("shard", None),
        P("shard", None),
        P("shard", None),
        P(),
        P(),
        P("shard", None, None),
        P("shard", None, None),
    )
    return jax.shard_map(
        on_device, mesh=mesh, in_specs=in_specs, out_specs=out_specs, check_vma=False
    )
```

profile of v0, /device:TPU:0, one launch (start us, length us, event | category | flops | bytes accessed | tf_op | source)
XLA Modules:
  0.0 1923.1 jit_solution(5788280154761019800)
XLA Ops:
  12.2 217.1 %gather_fusion = f32[65536,12]{1,0:T(8,128)} fusion(f32[383,12]{1,0:T(8,128)S(1)} %fusion.41, s32[65536]{0:T(1024)S(1)} %broadcast_clamp_fusion), kind=kCustom, calls=%fused_computation | custom fusion | bytes 6553600 | tf_op jit(solution)/shard_map/jit(_take)/gather | solution.py:45
  229.3 20.4 %copy.135 = f32[256,256,12]{0,1,2:T(8,128)} copy(f32[256,256,12]{2,1,0:T(8,128)} %bitcast.108) | data formatting | bytes 6291456 | tf_op jit(solution)/shard_map/jit(_take)/gather | solution.py:45
  257.7 5.2 gather_fusion.3
  293.4 165.9 %all-gather.17.cloned.1.call-done = bf16[4,768,3072]{2,1,0:T(8,128)(2,1)} async-done(((bf16[1,768,3072]{2,1,0:T(8,128)(2,1)}), bf16[4,768,3072]{2,1,0:T(8,128)(2,1)}) %all-gather.17.cloned.1.call-update) | async-done | bytes 18874384 | tf_op jit(solution)/shard_map/all_gather | solution.py:171
  459.3 15.3 fusion.15
  474.6 307.6 %all-gather.19.cloned.1.call-done = bf16[4,3072,768]{2,1,0:T(8,128)(2,1)} async-done(((bf16[1,3072,768]{2,1,0:T(8,128)(2,1)}), bf16[4,3072,768]{2,1,0:T(8,128)(2,1)}) %all-gather.19.cloned.1.call-update) | async-done | bytes 18874384 | tf_op jit(solution)/shard_map/all_gather | solution.py:172
  782.2 18.5 fusion.6
  800.7 11.9 convolution_convert_fusion.1
  812.7 14.5 convolution_convert_fusion
  829.0 11.1 convolution_convert_fusion.2
  844.9 15.1 convolution_convert_fusion.3
  869.7 24.4 %scatter_fusion = f32[256,4]{0,1:T(4,128)S(1)} fusion(f32[256,4]{0,1:T(4,128)S(1)} %broadcast_in_dim.55, s32[512]{0:T(512)S(1)} %reshape.401, f32[512]{0:T(512)S(1)} %reshape.403), kind=kCustom, calls=%fused_computation.9 | custom fusion | flops 512 | bytes 10240 | tf_op jit(solution)/shard_map/transpose(jvp(jit(take_along_axis)))/scatter-add | solution.py:78
  918.8 206.6 %reduce-scatter.29.cloned.1.call-done = bf16[1,768,3072]{2,1,0:T(8,128)(2,1)} async-done(((bf16[4,768,3072]{2,1,0:T(8,128)(2,1)}), bf16[1,768,3072]{2,1,0:T(8,128)(2,1)}) %reduce-scatter.29.cloned.1.call-update) | async-done | bytes 4718608 | tf_op jit(solution)/shard_map/reduce_scatter | solution.py:287
  1125.5 317.3 %reduce-scatter.33.cloned.1.call-done = bf16[1,3072,768]{2,1,0:T(8,128)(2,1)} async-done(((bf16[4,3072,768]{2,1,0:T(8,128)(2,1)}), bf16[1,3072,768]{2,1,0:T(8,128)(2,1)}) %reduce-scatter.33.cloned.1.call-update) | async-done | bytes 4718608 | tf_op jit(solution)/shard_map/reduce_scatter | solution.py:290
  1442.9 33.1 %reduce-scatter.21.cloned.1.call-done = bf16[192,768]{1,0:T(8,128)(2,1)} async-done(((bf16[768,768]{1,0:T(8,128)(2,1)}), bf16[192,768]{1,0:T(8,128)(2,1)}) %reduce-scatter.21.cloned.1.call-update) | async-done | bytes 294928 | tf_op jit(solution)/shard_map/reduce_scatter | solution.py:275
  1477.9 28.1 %reduce-scatter.23.cloned.1.call-done = bf16[192,768]{1,0:T(8,128)(2,1)} async-done(((bf16[768,768]{1,0:T(8,128)(2,1)}), bf16[192,768]{1,0:T(8,128)(2,1)}) %reduce-scatter.23.cloned.1.call-update) | async-done | bytes 294928 | tf_op jit(solution)/shard_map/reduce_scatter | solution.py:278
  1508.0 28.3 %reduce-scatter.25.cloned.1.call-done = bf16[192,768]{1,0:T(8,128)(2,1)} async-done(((bf16[768,768]{1,0:T(8,128)(2,1)}), bf16[192,768]{1,0:T(8,128)(2,1)}) %reduce-scatter.25.cloned.1.call-update) | async-done | bytes 294928 | tf_op jit(solution)/shard_map/reduce_scatter | solution.py:281
  1538.3 28.1 %reduce-scatter.27.cloned.1.call-done = bf16[192,768]{1,0:T(8,128)(2,1)} async-done(((bf16[768,768]{1,0:T(8,128)(2,1)}), bf16[192,768]{1,0:T(8,128)(2,1)}) %reduce-scatter.27.cloned.1.call-update) | async-done | bytes 294928 | tf_op jit(solution)/shard_map/reduce_scatter | solution.py:284
  1568.4 54.1 %reduce-scatter.31.cloned.1.call-done = bf16[1,96,3072]{2,1,0:T(8,128)(2,1)} async-done(((bf16[1,768,3072]{2,1,0:T(8,128)(2,1)}), bf16[1,96,3072]{2,1,0:T(8,128)(2,1)}) %reduce-scatter.31.cloned.1.call-update) | async-done | bytes 589840 | tf_op jit(solution)/shard_map/reduce_scatter | solution.py:307
  1622.6 57.6 %reduce-scatter.35.cloned.1.call-done = bf16[1,384,768]{2,1,0:T(8,128)(2,1)} async-done(((bf16[1,3072,768]{2,1,0:T(8,128)(2,1)}), bf16[1,384,768]{2,1,0:T(8,128)(2,1)}) %reduce-scatter.35.cloned.1.call-update) | async-done | bytes 589840 | tf_op jit(solution)/shard_map/reduce_scatter | solution.py:310
  1680.2 15.8 rev.4
  1708.9 9.2 reshape.328
  1726.7 40.3 %all-reduce.1 = (f32[768]{0:T(1024)}, f32[768]{0:T(1024)}, f32[32,12]{0,1:T(8,128)}, f32[768,4]{0,1:T(4,128)}) all-reduce(f32[768]{0:T(1024)S(1)} %get-tuple-element.52, f32[768]{0:T(1024)S(1)} %copy-done.52, f32[32,12]{0,1:T(8,128)S(1)} %copy-done.61, f32[768,4]{0,1:T(4,128)S(1)} %copy-done.38), channel_id=1, replica_groups=mesh['rep'=8,'shard'=4] {'rep','shard'}, use_global_device_ids=true, to_apply=%region_23.24 | all-reduce | flops 4992 | bytes 39936 | tf_op jit(solution)/shard_map/psum | solution.py:334
  1768.1 10.8 all_gather.48
  1779.9 9.3 all_gather.49
  1791.0 9.5 all_gather.50
  1801.4 26.3 %reduce-scatter.43.cloned.1.call-done = bf16[96,192]{1,0:T(8,128)(2,1)} async-done(((bf16[768,192]{1,0:T(8,128)(2,1)}), bf16[96,192]{1,0:T(8,128)(2,1)}) %reduce-scatter.43.cloned.1.call-update) | async-done | bytes 36880
  1827.7 9.5 all_gather.51
  1838.2 30.3 %all-gather.21.cloned.1.call-done = bf16[1,768,3072]{2,1,0:T(8,128)(2,1)} async-done(((bf16[1,96,3072]{2,1,0:T(8,128)(2,1)}), bf16[1,768,3072]{2,1,0:T(8,128)(2,1)}) %all-gather.21.cloned.1.call-update) | async-done | bytes 4718608 | tf_op jit(solution)/shard_map/all_gather | solution.py:327
  1868.6 7.4 convert_element_type.235
  1875.9 33.3 %all-gather.23.cloned.1.call-done = bf16[1,3072,768]{2,1,0:T(8,128)(2,1)} async-done(((bf16[1,384,768]{2,1,0:T(8,128)(2,1)}), bf16[1,3072,768]{2,1,0:T(8,128)(2,1)}) %all-gather.23.cloned.1.call-update) | async-done | bytes 4718608 | tf_op jit(solution)/shard_map/all_gather | solution.py:330
  1909.2 6.8 convert_element_type.237
  (292 shorter events, 118.5 us)
Async XLA Ops:
  7.2 256.0 %all-gather.9.cloned.1.call-start = ((), (), s32[]{:S(2)}) async-start(), calls=%async_computation.12 | async-start | bytes 1474560 | tf_op jit(solution)/shard_map/all_gather | solution.py:144
  7.9 257.4 %all-gather.11.cloned.1.call-start = ((), (), s32[]{:S(2)}) async-start(), calls=%async_computation.13 | async-start | bytes 1474560 | tf_op jit(solution)/shard_map/all_gather | solution.py:142
  8.7 258.7 %all-gather.13.cloned.1.call-start = ((), (), s32[]{:S(2)}) async-start(), calls=%async_computation.14 | async-start | bytes 1474560 | tf_op jit(solution)/shard_map/all_gather | solution.py:143
  9.4 265.6 %all-gather.15.cloned.1.call-start = ((), (), s32[]{:S(2)}) async-start(), calls=%async_computation.15 | async-start | bytes 1474560 | tf_op jit(solution)/shard_map/all_gather | solution.py:145
  10.0 449.3 %all-gather.17.cloned.1.call-start = ((), (), s32[]{:S(2)}) async-start(), calls=%async_computation.16 | async-start | bytes 23592960 | tf_op jit(solution)/shard_map/all_gather | solution.py:171
  10.6 771.6 %all-gather.19.cloned.1.call-start = ((), (), s32[]{:S(2)}) async-start(), calls=%async_computation.17 | async-start | bytes 23592960 | tf_op jit(solution)/shard_map/all_gather | solution.py:172
  11.2 1114.3 %reduce-scatter.29.cloned.1.call-start = ((), (), s32[]{:S(2)}) async-start(), calls=%async_computation.22 | async-start | bytes 23592960 | tf_op jit(solution)/shard_map/reduce_scatter | solution.py:287
  229.3 27.9 %copy-start.28 = (bf16[256,768]{1,0:T(8,128)(2,1)S(1)}, bf16[256,768]{1,0:T(8,128)(2,1)}, u32[]{:S(2)}) copy-start(bf16[256,768]{1,0:T(8,128)(2,1)} %param.16) | copy-start | bytes 1179652
  285.4 542.5 %copy-start.47 = (f32[256]{0:T(256)}, f32[256]{0:T(256)S(1)}, u32[]{:S(2)}) copy-start(f32[256]{0:T(256)S(1)} %fusion.63) | copy-start | bytes 3076
  812.6 630.2 %reduce-scatter.33.cloned.1.call-start = ((), (), s32[]{:S(2)}) async-start(), calls=%async_computation.25 | async-start | bytes 23592960 | tf_op jit(solution)/shard_map/reduce_scatter | solution.py:290
  827.3 648.7 %reduce-scatter.21.cloned.1.call-start = ((), (), s32[]{:S(2)}) async-start(), calls=%async_computation.18 | async-start | bytes 1474560 | tf_op jit(solution)/shard_map/reduce_scatter | solution.py:275
  869.6 24.6 %copy-start.11 = (f32[256,768]{1,0:T(8,128)S(1)}, f32[256,768]{1,0:T(8,128)}, u32[]{:S(2)}) copy-start(f32[256,768]{1,0:T(8,128)} %copy-done.10) | copy-start | bytes 2359300
  869.7 24.6 %copy-start.45 = (f32[768]{0:T(1024)S(1)}, f32[768]{0:T(1024)}, u32[]{:S(2)}) copy-start(f32[768]{0:T(1024)} %param.21) | copy-start | bytes 9220
  869.7 24.6 %copy-start.48 = (f32[256]{0:T(256)S(1)}, f32[256]{0:T(256)}, u32[]{:S(2)}) copy-start(f32[256]{0:T(256)} %copy-done.47) | copy-start | bytes 3076
  869.7 24.6 %copy-start.51 = (bf16[768,4]{0,1:T(4,128)(2,1)S(1)}, bf16[768,4]{0,1:T(4,128)(2,1)}, u32[]{:S(2)}) copy-start(bf16[768,4]{0,1:T(4,128)(2,1)} %param.27) | copy-start | bytes 18436
  869.7 24.5 %copy-start.54 = (f32[256]{0:T(256)S(1)}, f32[256]{0:T(256)}, u32[]{:S(2)}) copy-start(f32[256]{0:T(256)} %copy-done.53) | copy-start | bytes 3076
  869.7 25.9 %copy-start.58 = (f32[256]{0:T(256)S(1)}, f32[256]{0:T(256)}, u32[]{:S(2)}) copy-start(f32[256]{0:T(256)} %copy-done.57) | copy-start | bytes 3076
  869.7 25.9 %copy-start.29 = (bf16[256,768]{1,0:T(8,128)(2,1)S(1)}, bf16[256,768]{1,0:T(8,128)(2,1)}, u32[]{:S(2)}) copy-start(bf16[256,768]{1,0:T(8,128)(2,1)} %param.16) | copy-start | bytes 1179652
  908.4 597.7 %reduce-scatter.23.cloned.1.call-start = ((), (), s32[]{:S(2)}) async-start(), calls=%async_computation.19 | async-start | bytes 1474560 | tf_op jit(solution)/shard_map/reduce_scatter | solution.py:278
  913.0 623.3 %reduce-scatter.25.cloned.1.call-start = ((), (), s32[]{:S(2)}) async-start(), calls=%async_computation.20 | async-start | bytes 1474560 | tf_op jit(solution)/shard_map/reduce_scatter | solution.py:281
  917.1 649.3 %reduce-scatter.27.cloned.1.call-start = ((), (), s32[]{:S(2)}) async-start(), calls=%async_computation.21 | async-start | bytes 1474560 | tf_op jit(solution)/shard_map/reduce_scatter | solution.py:284
  918.8 703.7 %reduce-scatter.31.cloned.1.call-start = ((), (), s32[]{:S(2)}) async-start(), calls=%async_computation.23 | async-start | bytes 5308416 | tf_op jit(solution)/shard_map/reduce_scatter | solution.py:307
  1125.5 554.7 %reduce-scatter.35.cloned.1.call-start = ((), (), s32[]{:S(2)}) async-start(), calls=%async_computation.26 | async-start | bytes 5308416 | tf_op jit(solution)/shard_map/reduce_scatter | solution.py:310
  1442.8 237.3 %copy-start.7 = (bf16[12,256,256]{1,2,0:T(8,128)(2,1)S(1)}, bf16[12,256,256]{1,2,0:T(8,128)(2,1)}, u32[]{:S(2)}) copy-start(bf16[12,256,256]{1,2,0:T(8,128)(2,1)} %copy-done.6) | copy-start | bytes 4718596
  1442.8 325.3 %reduce-scatter.37.cloned.1.call-start = ((), (), s32[]{:S(2)}) async-start(), calls=%async_computation.28 | async-start | bytes 442368
  1477.9 302.0 %reduce-scatter.39.cloned.1.call-start = ((), (), s32[]{:S(2)}) async-start(), calls=%async_computation.29 | async-start | bytes 442368
  1508.0 283.0 %reduce-scatter.41.cloned.1.call-start = ((), (), s32[]{:S(2)}) async-start(), calls=%async_computation.30 | async-start | bytes 442368
  1538.2 289.5 %reduce-scatter.43.cloned.1.call-start = ((), (), s32[]{:S(2)}) async-start(), calls=%async_computation.31 | async-start | bytes 442368
  1568.3 300.2 %all-gather.21.cloned.1.call-start = ((), (), s32[]{:S(2)}) async-start(), calls=%async_computation.24 | async-start | bytes 5308416 | tf_op jit(solution)/shard_map/all_gather | solution.py:327
  1622.5 286.7 %all-gather.23.cloned.1.call-start = ((), (), s32[]{:S(2)}) async-start(), calls=%async_computation.27 | async-start | bytes 5308416 | tf_op jit(solution)/shard_map/all_gather | solution.py:330
  1725.4 41.6 %copy-start.14 = (f32[256,768]{1,0:T(8,128)S(1)}, f32[256,768]{1,0:T(8,128)}, u32[]{:S(2)}) copy-start(f32[256,768]{1,0:T(8,128)} %copy-done.12) | copy-start | bytes 2359300
  1726.0 41.0 %copy-start.60 = (f32[256]{0:T(256)S(1)}, f32[256]{0:T(256)}, u32[]{:S(2)}) copy-start(f32[256]{0:T(256)} %copy-done.59) | copy-start | bytes 3076
  (54 other events, 261.0 us)
Sparse Core Ops, SparseCore 0:
  9.6 33.1 all-gather.8
  44.3 29.5 all-gather.10
  75.5 29.5 all-gather.12
  106.5 29.5 all-gather.14
  137.5 321.7 all-gather.16
  460.7 321.4 all-gather.18
  812.8 312.6 reduce-scatter.28
  1127.9 314.8 reduce-scatter.32
  1445.7 30.2 reduce-scatter.20
  1478.1 27.8 reduce-scatter.22
  1508.4 27.8 reduce-scatter.24
  1538.5 27.8 reduce-scatter.26
  1569.8 52.5 reduce-scatter.30
  1626.2 53.8 reduce-scatter.34
  1683.6 33.7 reduce-scatter.36
  1720.3 33.7 reduce-scatter.38
  1757.1 33.8 reduce-scatter.40
  1793.9 33.8 reduce-scatter.42
  1829.6 38.8 all-gather.20
  1870.3 38.9 all-gather.22
where the time goes:
time: 1930 us; the launch traced here: 1920 us
  waiting for transfers between devices  1320 us (68%)
  local copies, waits for them, and re-layouts  330 us (17%)
  matrix products  118 us (6%)
  blocking collectives  79.3 us (4%)
  other arithmetic  56.7 us (3%)
    reduce_scatter x1, waiting for transfers between devices, on_device(): lax.psum_scatter(whole_second.astype(jnp.bfloat16), 'shard', scatter_dime...  317 us
    all_gather x1, waiting for transfers between devices, on_device(): lax.all_gather(w_down, 'shard', axis=0, tiled=True)  308 us
    gather x2, local copies, waits for them, and re-layouts, position_bias(): return jnp.transpose(jnp.take(per_gap, offset, axis=0), (2, 0, 1))  237 us
    reduce_scatter x1, waiting for transfers between devices, on_device(): lax.psum_scatter(whole_first.astype(jnp.bfloat16), 'shard', scatter_dimen...  207 us
    all_gather x1, waiting for transfers between devices, on_device(): lax.all_gather(w_in, 'shard', axis=0, tiled=True)  166 us
    reduce_scatter x1, waiting for transfers between devices, on_device(): lax.psum_scatter(own_second.astype(jnp.bfloat16), 'rep', scatter_dimensio...  57.6 us
    reduce_scatter x1, waiting for transfers between devices, on_device(): lax.psum_scatter(own_first.astype(jnp.bfloat16), 'rep', scatter_dimension...  54.1 us
    psum x1, blocking collectives, on_device(): lax.psum((grad_gain_attn, grad_gain_moe, grad_table, grad_router), ('rep'...  40.3 us
  transfers between devices with their start and end apart: 20, of which 14 were waited for; matrix products, arithmetic and copies ran while one was open for 24% of the time, Pallas kernels for 0%

commit v1 on v0

v1 whole, which is shorter than its diff:
```python
import functools

import jax
import jax.numpy as jnp
from jax import lax
from jax.experimental import pallas as pl
from jax.experimental.pallas import tpu as pltpu
from jax.sharding import PartitionSpec as P

HEADS = 12
HEAD_DIM = 64
EPS = 1e-06
LOW = jnp.bfloat16


def product(left, right):
    return jnp.dot(left, right, preferred_element_type=jnp.float32)


def inner_left(left, right):
    return lax.dot_general(
        left, right, (((0,), (0,)), ((), ())), preferred_element_type=jnp.float32
    )


def inner_right(left, right):
    return lax.dot_general(
        left, right, (((1,), (1,)), ((), ())), preferred_element_type=jnp.float32
    )


def inverse_rms(features):
    return lax.rsqrt(jnp.mean(features * features, axis=-1, keepdims=True) + EPS)


def rms_pull(features, scale, gain_vec, grad):
    unit = features * scale
    scaled = grad * gain_vec
    grad_features = scale * (scaled - unit * jnp.mean(scaled * unit, axis=-1, keepdims=True))
    return grad_features, jnp.sum(grad * unit, axis=0)


def gap_onehot(buckets, count, width):
    span = (buckets.shape[0] + 1) // 2
    back = jnp.flip(buckets)
    lanes = jnp.concatenate(
        [back[span - 1 :], jnp.full((width - 2 * span + 1,), -1, jnp.int32), back[: span - 1]]
    )
    return (lanes[:, None] == jnp.arange(count, dtype=jnp.int32)[None, :]).astype(jnp.float32)


def sum_onehot(buckets, count, width):
    ahead = width // 2 - (buckets.shape[0] + 1) // 2
    lanes = jnp.pad(
        buckets, (ahead, width - ahead - buckets.shape[0]), constant_values=-1
    )
    return (lanes[:, None] == jnp.arange(count, dtype=jnp.int32)[None, :]).astype(jnp.float32)


def attention_kernel(q_ref, k_ref, v_ref, gap_ref, col_ref, row_ref, p_ref, o_ref):
    rows = q_ref.shape[0]
    same = col_ref[...] == row_ref[...]
    for s in range(2):
        cols = pl.ds(s * HEAD_DIM, HEAD_DIM)
        skew = pltpu.roll(
            jnp.broadcast_to(gap_ref[s], (rows, gap_ref.shape[2])), 0, 1, stride=1, stride_axis=0
        )[:, :rows]
        scores = inner_right(q_ref[:, cols], k_ref[:, cols]) * HEAD_DIM ** (-0.5)
        scores = jnp.where(same, scores + skew, -1e30)
        grown = jnp.exp(scores - jnp.max(scores, axis=-1, keepdims=True))
        probs = grown / jnp.sum(grown, axis=-1, keepdims=True)
        p_ref[s] = probs
        o_ref[:, cols] = product(probs.astype(LOW), v_ref[:, cols]).astype(LOW)


def attention(qkv, gaps, doc_row):
    rows = qkv.shape[0]
    width = gaps.shape[2]
    pairs = HEADS // 2
    two = 2 * HEAD_DIM

    def part(n):
        return pl.BlockSpec((rows, two), lambda h: (0, n * pairs + h))

    return pl.pallas_call(
        attention_kernel,
        grid=(pairs,),
        in_specs=[
            part(0),
            part(1),
            part(2),
            pl.BlockSpec((2, 1, width), lambda h: (h, 0, 0)),
            pl.BlockSpec((rows, 1), lambda h: (0, 0)),
            pl.BlockSpec((1, rows), lambda h: (0, 0)),
        ],
        out_specs=[pl.BlockSpec((2, rows, rows), lambda h: (h, 0, 0)), part(0)],
        out_shape=[
            jax.ShapeDtypeStruct((HEADS, rows, rows), jnp.float32),
            jax.ShapeDtypeStruct((rows, HEADS * HEAD_DIM), LOW),
        ],
        compiler_params=pltpu.CompilerParams(vmem_limit_bytes=32 * 1024 * 1024),
        cost_estimate=pl.CostEstimate(
            flops=4 * HEADS * rows * rows * HEAD_DIM,
            bytes_accessed=4 * HEADS * rows * rows,
            transcendentals=HEADS * rows * rows,
        ),
    )(qkv, qkv, qkv, gaps, doc_row.reshape(-1, 1), doc_row.reshape(1, -1))


def attention_back_kernel(q_ref, k_ref, v_ref, p_ref, g_ref, gq_ref, gk_ref, gv_ref, gap_ref):
    rows = q_ref.shape[0]
    width = gap_ref.shape[2]
    scale = HEAD_DIM ** (-0.5)
    down = lax.broadcasted_iota(jnp.int32, (rows, rows), 0)
    across = lax.broadcasted_iota(jnp.int32, (rows, rows), 1)
    mirror = (down + across == rows - 1).astype(LOW)
    for s in range(2):
        cols = pl.ds(s * HEAD_DIM, HEAD_DIM)
        probs = p_ref[s]
        out_grad = g_ref[:, cols]
        grad_p = inner_right(out_grad, v_ref[:, cols])
        gv_ref[:, cols] = inner_left(probs.astype(LOW), out_grad).astype(LOW)
        grad_s = probs * (grad_p - jnp.sum(grad_p * probs, axis=-1, keepdims=True))
        grad_low = grad_s.astype(LOW)
        gq_ref[:, cols] = (product(grad_low, k_ref[:, cols]) * scale).astype(LOW)
        gk_ref[:, cols] = (inner_left(grad_low, q_ref[:, cols]) * scale).astype(LOW)
        wide = jnp.concatenate(
            [product(grad_low, mirror), jnp.zeros((rows, width - rows), jnp.float32)], axis=1
        )
        straight = pltpu.roll(wide, 0, 1, stride=1, stride_axis=0)
        gap_ref[s] = jnp.sum(straight, axis=0, keepdims=True)


def attention_back(qkv, probs, grad_heads, width):
    rows = qkv.shape[0]
    pairs = HEADS // 2
    two = 2 * HEAD_DIM

    def part(n):
        return pl.BlockSpec((rows, two), lambda h: (0, n * pairs + h))

    flat = jax.ShapeDtypeStruct((rows, HEADS * HEAD_DIM), LOW)
    return pl.pallas_call(
        attention_back_kernel,
        grid=(pairs,),
        in_specs=[
            part(0),
            part(1),
            part(2),
            pl.BlockSpec((2, rows, rows), lambda h: (h, 0, 0)),
            part(0),
        ],
        out_specs=[
            part(0),
            part(0),
            part(0),
            pl.BlockSpec((2, 1, width), lambda h: (h, 0, 0)),
        ],
        out_shape=[flat, flat, flat, jax.ShapeDtypeStruct((HEADS, 1, width), jnp.float32)],
        compiler_params=pltpu.CompilerParams(vmem_limit_bytes=32 * 1024 * 1024),
        cost_estimate=pl.CostEstimate(
            flops=8 * HEADS * rows * rows * HEAD_DIM,
            bytes_accessed=4 * HEADS * rows * rows,
            transcendentals=0,
        ),
    )(qkv, qkv, qkv, probs, grad_heads)


def gather_projections(stacked, rep, piece):
    part = lax.dynamic_slice_in_dim(stacked, rep * piece, piece, axis=0)
    return lax.all_gather(part, ("shard", "rep"), axis=0, tiled=True)


def reduce_projections(whole):
    return lax.psum_scatter(whole, ("shard", "rep"), scatter_dimension=0, tiled=True)


def on_device(
    tokens,
    cotangent,
    doc_ids,
    buckets,
    routes,
    gain_attn,
    gain_moe,
    w_query,
    w_key,
    w_value,
    w_proj,
    rel_table,
    w_router,
    w_in,
    w_down,
):
    rows_here, model = tokens.shape
    reps = lax.axis_size("rep")
    rep = lax.axis_index("rep")
    mine = lax.axis_index("shard")
    width = 2 * rows_here
    inputs = tokens.astype(jnp.float32)

    stacked = jnp.concatenate([w_query, w_key, w_value, w_proj], axis=1)
    piece = stacked.shape[0] // reps
    full = gather_projections(stacked, rep, piece)
    all_cot = lax.all_gather(cotangent, "shard", axis=0, tiled=True)
    all_routes = lax.all_gather(routes, "shard", axis=0, tiled=True)

    onehot = gap_onehot(buckets, rel_table.shape[0], width)
    gaps = lax.dot_general(
        rel_table, onehot, (((0,), (1,)), ((), ())), precision=lax.Precision.HIGHEST
    ).reshape(HEADS, 1, width)
    scale_first = inverse_rms(inputs)
    h_first = (inputs * scale_first * gain_attn).astype(LOW)
    full_qkv = full[:, : 3 * model]
    full_proj = full[:, 3 * model :]
    qkv = product(h_first, full_qkv).astype(LOW)
    probs, mixed_heads = attention(qkv, gaps, doc_ids[0])
    y_first = inputs + product(mixed_heads, full_proj)
    scale_second = inverse_rms(y_first)
    h_second = (y_first * scale_second * gain_moe).astype(LOW)

    all_h = lax.all_gather(h_second, "shard", axis=0, tiled=True)
    logits = product(all_h, w_router)
    ids = jnp.arange(w_router.shape[1], dtype=jnp.int32)[None, :]
    hot_first = (all_routes[:, 0:1] == ids).astype(jnp.float32)
    hot_second = (all_routes[:, 1:2] == ids).astype(jnp.float32)
    apart = hot_first - hot_second
    gap_logit = jnp.sum(logits * apart, axis=1, keepdims=True)
    gate_first = jax.nn.sigmoid(gap_logit)
    gate_second = jax.nn.sigmoid(-gap_logit)
    is_first = (all_routes[:, 0:1] == mine).astype(jnp.float32)
    is_second = (all_routes[:, 1:2] == mine).astype(jnp.float32)
    gate = is_first * gate_first + is_second * gate_second
    out_grad_all = all_cot.astype(jnp.float32)
    grad_eo = (out_grad_all * gate).astype(LOW)

    w_first, w_second = w_in[0], w_down[0]
    hidden = product(all_h, w_first)
    act_full, gelu_pull = jax.vjp(jax.nn.gelu, hidden)
    act_low = act_full.astype(LOW)
    grad_act = inner_right(grad_eo, w_second)
    grad_hidden = gelu_pull(grad_act)[0].astype(LOW)
    expert_out = product(act_low, w_second).astype(LOW).astype(jnp.float32)
    grad_rows = inner_right(grad_hidden, w_first)
    grad_gate = jnp.sum(out_grad_all * expert_out, axis=1, keepdims=True)
    grad_gap = grad_gate * (is_first - is_second) * gate_first * gate_second
    grad_logits = grad_gap * apart
    grad_router = lax.dot_general(
        all_h.astype(jnp.float32),
        grad_logits,
        (((0,), (0,)), ((), ())),
        precision=lax.Precision.HIGHEST,
    )
    back_h = grad_rows + lax.dot_general(
        grad_logits,
        w_router.astype(jnp.float32),
        (((1,), (1,)), ((), ())),
        precision=lax.Precision.HIGHEST,
    )
    grad_h_second = lax.psum_scatter(
        back_h.astype(LOW), "shard", scatter_dimension=0, tiled=True
    ).astype(jnp.float32)

    grad_down = inner_left(act_low, grad_eo).astype(LOW)
    grad_in = inner_left(all_h, grad_hidden).astype(LOW)
    part_down = lax.psum_scatter(grad_down, "rep", scatter_dimension=0, tiled=True)
    part_in = lax.psum_scatter(grad_in, "rep", scatter_dimension=0, tiled=True)
    routed = lax.psum_scatter(
        (gate * expert_out).astype(LOW), "shard", scatter_dimension=0, tiled=True
    ).astype(jnp.float32)
    mixed = (y_first + routed).astype(LOW)

    out_grad = cotangent.astype(jnp.float32)
    grad_y_part, grad_gain_moe = rms_pull(y_first, scale_second, gain_moe, grad_h_second)
    grad_y_first = out_grad + grad_y_part
    grad_attn = grad_y_first.astype(LOW)
    grad_heads = inner_right(grad_attn, full_proj).astype(LOW)
    grad_q, grad_k, grad_v, grad_gap_sums = attention_back(qkv, probs, grad_heads, width)
    grad_table = lax.dot_general(
        sum_onehot(buckets, rel_table.shape[0], width),
        grad_gap_sums.reshape(HEADS, width),
        (((0,), (1,)), ((), ())),
        precision=lax.Precision.HIGHEST,
    )
    grad_qkv = jnp.concatenate([grad_q, grad_k, grad_v], axis=1)
    grad_h_first = inner_right(grad_qkv, full_qkv)
    whole = jnp.concatenate(
        [inner_left(h_first, grad_qkv).astype(LOW), inner_left(mixed_heads, grad_attn).astype(LOW)],
        axis=1,
    )
    own = reduce_projections(whole)
    grad_x_part, grad_gain_attn = rms_pull(inputs, scale_first, gain_attn, grad_h_first)
    grad_tokens = grad_y_first + grad_x_part

    sum_down = lax.all_gather(part_down, "rep", axis=0, tiled=True).astype(jnp.float32)
    sum_in = lax.all_gather(part_in, "rep", axis=0, tiled=True).astype(jnp.float32)
    own = lax.all_gather(own, "rep", axis=0, tiled=True).astype(jnp.float32)
    small = jnp.concatenate(
        [
            grad_gain_attn,
            grad_gain_moe,
            grad_router.reshape(-1),
            grad_table.reshape(-1),
        ]
    )
    cut = small.shape[0]
    lines = -(-cut // 1024) * 8
    small = jnp.pad(small, (0, lines * 128 - cut)).reshape(lines, 128)
    small = lax.psum(small, ("rep", "shard")).reshape(-1)
    marks = [model, 2 * model, 2 * model + w_router.size]
    sum_gain_attn, sum_gain_moe, sum_router, sum_table = jnp.split(small[:cut], marks)
    return (
        mixed,
        grad_tokens,
        sum_gain_attn,
        sum_gain_moe,
        own[:, :model],
        own[:, model : 2 * model],
        own[:, 2 * model : 3 * model],
        own[:, 3 * model :],
        sum_table.reshape(rel_table.shape),
        sum_router.reshape(w_router.shape),
        sum_in[None],
        sum_down[None],
    )


def solution(mesh):
    in_specs = (
        P(("rep", "shard"), None),
        P(("rep", "shard"), None),
        P(("rep", "shard"), None),
        P(),
        P(("rep", "shard"), None),
        P(),
        P(),
        P("shard", None),
        P("shard", None),
        P("shard", None),
        P("shard", None),
        P(),
        P(),
        P("shard", None, None),
        P("shard", None, None),
    )
    out_specs = (
        P(("rep", "shard"), None),
        P(("rep", "shard"), None),
        P(),
        P(),
        P("shard", None),
        P("shard", None),
        P("shard", None),
        P("shard", None),
        P(),
        P(),
        P("shard", None, None),
        P("shard", None, None),
    )
    return jax.shard_map(
        on_device, mesh=mesh, in_specs=in_specs, out_specs=out_specs, check_vma=False
    )
```

time: 1930 us -> 638 us (0.33)
  waiting for transfers between devices: 1320 us -> 428 us
  local copies, waits for them, and re-layouts: 330 us -> 11.1 us
  matrix products: 118 us -> 87.6 us
  other arithmetic: 56.7 us -> 26.8 us
  blocking collectives: 79.3 us -> 51.9 us
    reduce_scatter x8 -> x5, waiting for transfers between devices: 753 us -> 265 us  [the longest x1 83.6 us: reduce_projections(): lax.psum_scatter(whole, ('shard', 'rep'), scatter_dimension=0, tiled=True)]
    all_gather x8 -> x6, waiting for transfers between devices: 537 us -> 161 us  [the longest x1 64.8 us: gather_projections(): return lax.all_gather(part, ('shard', 'rep'), axis=0, tiled=True)]
    gather x14 -> x0, local copies, waits for them, and re-layouts: 260 us -> none  [the longest x2 237 us: position_bias(): return jnp.transpose(jnp.take(per_gap, offset, axis=0), (2, 0, 1))]
    dot_general x16 -> x4, matrix products: 99.8 us -> 6.52 us  [the longest x1 3.15 us: on_device(): lax.dot_general(all_h.astype(jnp.float32), grad_logits, (((0,), (0,)), ((...]
    unnamed x24 -> x11, waiting for transfers between devices: 31 us -> 1.36 us
    all_gather x4 -> x1, blocking collectives: 39.1 us -> 12.2 us  [on_device(): all_routes = lax.all_gather(routes, 'shard', axis=0, tiled=True)]
    scatter-add x1 -> x0, other arithmetic: 24.4 us -> none  [gate_values(): picked = jnp.take_along_axis(expert_probs, route_row, axis=1)]
    dot_general x4, matrix products: 4.24 us -> 27.5 us  [inner_right(): lax.dot_general(left, right, (((1,), (1,)), ((), ())), preferred_element_...]
  transfers between devices with their start and end apart: 20 -> 11, of which waited for: 14 -> 10; matrix products, arithmetic and copies ran while one was open for 24% -> 10% of each run, Pallas kernels for 0% -> 0%
where the time goes in v1:
time: 638 us; the launch traced here: 637 us
  waiting for transfers between devices  428 us (67%)
  matrix products  87.6 us (14%)
  blocking collectives  51.9 us (8%)
  other arithmetic  26.8 us (4%)
  Pallas kernels  16.8 us (3%)
  between operations  14.3 us (2%)
  local copies, waits for them, and re-layouts  11.1 us (2%)
    reduce_scatter x1, waiting for transfers between devices, reduce_projections(): lax.psum_scatter(whole, ('shard', 'rep'), scatter_dimension=0, tiled=True)  83.6 us
    all_gather x1, waiting for transfers between devices, gather_projections(): return lax.all_gather(part, ('shard', 'rep'), axis=0, tiled=True)  64.8 us
    reduce_scatter x1, waiting for transfers between devices, on_device(): lax.psum_scatter(grad_down, 'rep', scatter_dimension=0, tiled=True)  57.6 us
    reduce_scatter x1, waiting for transfers between devices, on_device(): part_in = lax.psum_scatter(grad_in, 'rep', scatter_dimension=0, tiled=True)  56.8 us
    psum x1, blocking collectives, on_device(): small = lax.psum(small, ('rep', 'shard')).reshape(-1)  39.7 us
    reduce_scatter x1, waiting for transfers between devices, on_device(): lax.psum_scatter((gate * expert_out).astype(LOW), 'shard', scatter_dimens...  33.9 us
    all_gather x1, waiting for transfers between devices, on_device(): lax.all_gather(part_down, 'rep', axis=0, tiled=True).astype(jnp.float32)  33.6 us
    reduce_scatter x1, waiting for transfers between devices, on_device(): lax.psum_scatter(back_h.astype(LOW), 'shard', scatter_dimension=0, tiled=...  33.4 us
  transfers between devices with their start and end apart: 11, of which 10 were waited for; matrix products, arithmetic and copies ran while one was open for 10% of the time, Pallas kernels for 0%

profile of v1, /device:TPU:0, one launch (start us, length us, event | category | flops | bytes accessed | tf_op | source)
XLA Modules:
  0.0 637.4 jit_solution(2422550807566416659)
XLA Ops:
  13.1 64.8 %all-gather.7.cloned.1.call-done = bf16[768,3072]{1,0:T(8,128)(2,1)} async-done(((bf16[24,3072]{1,0:T(8,128)(2,1)}), bf16[768,3072]{1,0:T(8,128)(2,1)}) %all-gather.7.cloned.1.call-update) | async-done | bytes 4718608 | tf_op jit(solution)/shard_map/all_gather | solution.py:171
  77.9 3.3 convolution_convert_fusion.3.q_ref.k_ref.v_ref
  81.2 9.5 %shard_map.238 = (f32[12,256,256]{2,1,0:T(8,128)S(1)}, bf16[256,768]{1,0:T(8,128)(2,1)S(1)}) custom-call(bf16[256,2304]{1,0:T(8,128)(2,1)S(1)} %convolution_convert_fusion.3.q_ref.k_ref.v_ref, bf16[256,2304]{1,0:T(8,128)(2,1)S(1)} %convolution_convert_fusion.3.q_ref.k_ref.v_ref, bf16[256,2304]{1,0:T(8,128)(2,1)S(1)} %convolution_convert_fusion.3.q_ref.k_ref.v_ref, ...), custom_call_target="tpu_custom_call" | custom-call | flops 201326592 | bytes 3145728 | tf_op jit(solution)/shard_map/pallas_call | solution.py:85
  92.4 1.8 multiply_reduce_fusion
  96.0 12.2 %all_gather.22 = s32[1024,2]{0,1:T(2,128)S(1)} all-gather(s32[256,2]{0,1:T(2,128)S(1)} %copy-done.16), channel_id=1, replica_groups=mesh['rep'=8,'shard'=4] {'shard'}, dimensions={0}, use_global_device_ids=true | all-gather | bytes 10240 | tf_op jit(solution)/shard_map/all_gather | solution.py:206
  108.2 23.1 %all-gather.9.cloned.1.call-done = bf16[1024,768]{1,0:T(8,128)(2,1)} async-done(((bf16[256,768]{1,0:T(8,128)(2,1)}), bf16[1024,768]{1,0:T(8,128)(2,1)}) %all-gather.9.cloned.1.call-update) | async-done | bytes 1572880 | tf_op jit(solution)/shard_map/all_gather | solution.py:222
  131.3 1.9 fusion.30
  133.3 10.0 %fusion.13 = f32[1024,3072]{1,0:T(8,128)} fusion(bf16[1024,768]{1,0:T(8,128)(2,1)} %all-gather.9.cloned.1.call-done, bf16[1,768,3072]{2,1,0:T(8,128)(2,1)} %param.28), kind=kOutput, calls=%fused_computation.22 | convolution fusion | flops 4831838208 | bytes 18874368 | tf_op jit(solution)/shard_map/dot_general | solution.py:17
  143.3 25.6 %all-gather.11.cloned.1.call-done = bf16[1024,768]{1,0:T(8,128)(2,1)} async-done(((bf16[256,768]{1,0:T(8,128)(2,1)}), bf16[1024,768]{1,0:T(8,128)(2,1)}) %all-gather.11.cloned.1.call-update) | async-done | bytes 1572880 | tf_op jit(solution)/shard_map/all_gather | solution.py:205
  168.8 13.1 %fusion.19 = (f32[1024]{0:T(1024)S(1)}, bf16[1024,768]{1,0:T(8,128)(2,1)}) fusion(bf16[1024,768]{1,0:T(8,128)(2,1)} %all-gather.11.cloned.1.call-done, f32[1024]{0:T(1024)S(1)} %bitcast.72, bf16[1,3072,768]{2,1,0:T(8,128)(2,1)} %param.29, f32[1024,3072]{1,0:T(8,128)} %fusion.13), kind=kOutput, calls=%fused_computation.30 | convolution fusion | flops 4865653760 | bytes 20455424 | tf_op jit(solution)/shard_map/dot_general | solution.py:17
  182.0 15.3 %fusion.6 = bf16[1024,3072]{1,0:T(8,128)(2,1)} fusion(f32[1024,3072]{1,0:T(8,128)} %fusion.13, bf16[1,3072,768]{2,1,0:T(8,128)(2,1)} %param.29, bf16[1024,768]{1,0:T(8,128)(2,1)S(1)} %copy-done.17, f32[1024]{0:T(1024)S(1)} %bitcast.73), kind=kOutput, calls=%fused_computation.8 | convolution fusion | flops 4897112064 | bytes 25169920 | tf_op jit(solution)/shard_map/dot_general | solution.py:27
  197.3 7.2 %fusion.11 = f32[1024,768]{1,0:T(8,128)S(1)} fusion(bf16[1024,3072]{1,0:T(8,128)(2,1)} %fusion.6, bf16[1,768,3072]{2,1,0:T(8,128)(2,1)S(1)} %bitcast.76), kind=kOutput, calls=%fused_computation.20 | convolution fusion | flops 4831838208 | bytes 14155776 | tf_op jit(solution)/shard_map/dot_general | solution.py:27
  204.5 2.7 add_convert_fusion
  208.1 33.4 %reduce-scatter.8.cloned.1.call-done = bf16[256,768]{1,0:T(8,128)(2,1)} async-done(((bf16[1024,768]{1,0:T(8,128)(2,1)}), bf16[256,768]{1,0:T(8,128)(2,1)}) %reduce-scatter.8.cloned.1.call-update) | async-done | bytes 393232 | tf_op jit(solution)/shard_map/reduce_scatter | solution.py:260
  241.5 1.9 fusion.38
  244.0 33.9 %reduce-scatter.6.cloned.1.call-done = bf16[256,768]{1,0:T(8,128)(2,1)} async-done(((bf16[1024,768]{1,0:T(8,128)(2,1)}), bf16[256,768]{1,0:T(8,128)(2,1)}) %reduce-scatter.6.cloned.1.call-update) | async-done | bytes 393232 | tf_op jit(solution)/shard_map/reduce_scatter | solution.py:268
  278.0 2.4 fusion.37
  282.7 7.3 %shard_map.239 = (bf16[256,768]{1,0:T(8,128)(2,1)S(1)}, bf16[256,768]{1,0:T(8,128)(2,1)S(1)}, bf16[256,768]{1,0:T(8,128)(2,1)S(1)}, f32[12,1,512]{2,1,0:T(1,128)S(1)}) custom-call(bf16[256,2304]{1,0:T(8,128)(2,1)S(1)} %convolution_convert_fusion.3.q_ref.k_ref.v_ref, bf16[256,2304]{1,0:T(8,128)(2,1)S(1)} %convolution_convert_fusion.3.q_ref.k_ref.v_ref, ...), custom_call_target="tpu_custom_call" | custom-call | flops 402653184 | bytes 3145728 | tf_op jit(solution)/shard_map/pallas_call | solution.py:143
  291.4 2.8 pad_maximum_fusion
  294.3 9.1 %convolution_convert_fusion.1 = bf16[768,3072]{1,0:T(8,128)(2,1)} fusion(bf16[1024,768]{1,0:T(8,128)(2,1)} %all-gather.9.cloned.1.call-done, bf16[1024,3072]{1,0:T(8,128)(2,1)} %fusion.6), kind=kOutput, calls=%fused_computation.11 | convolution fusion | flops 4834197504 | bytes 12582912 | tf_op jit(solution)/shard_map/dot_general | solution.py:21
  304.1 12.6 %convolution_convert_fusion = bf16[3072,768]{1,0:T(8,128)(2,1)} fusion(bf16[1024,768]{1,0:T(8,128)(2,1)} %all-gather.11.cloned.1.call-done, f32[1024]{0:T(1024)S(1)} %bitcast.74, f32[1024,3072]{1,0:T(8,128)} %fusion.13), kind=kOutput, calls=%fused_computation.10 | convolution fusion | flops 4864868352 | bytes 18878464 | tf_op jit(solution)/shard_map/dot_general | solution.py:21
  316.8 83.6 %reduce-scatter.10.cloned.1.call-done = bf16[24,3072]{1,0:T(8,128)(2,1)} async-done(((bf16[768,3072]{1,0:T(8,128)(2,1)}), bf16[24,3072]{1,0:T(8,128)(2,1)}) %reduce-scatter.10.cloned.1.call-update) | async-done | bytes 147472 | tf_op jit(solution)/shard_map/reduce_scatter | solution.py:175
  400.4 56.8 %reduce-scatter.12.cloned.1.call-done = bf16[96,3072]{1,0:T(8,128)(2,1)} async-done(((bf16[768,3072]{1,0:T(8,128)(2,1)}), bf16[96,3072]{1,0:T(8,128)(2,1)}) %reduce-scatter.12.cloned.1.call-update) | async-done | bytes 589840 | tf_op jit(solution)/shard_map/reduce_scatter | solution.py:267
  457.6 57.6 %reduce-scatter.14.cloned.1.call-done = bf16[384,768]{1,0:T(8,128)(2,1)} async-done(((bf16[3072,768]{1,0:T(8,128)(2,1)}), bf16[384,768]{1,0:T(8,128)(2,1)}) %reduce-scatter.14.cloned.1.call-update) | async-done | bytes 589840 | tf_op jit(solution)/shard_map/reduce_scatter | solution.py:266
  515.3 3.2 fusion.64
  519.2 3.2 fusion.44
  522.4 39.7 %psum.7 = f32[40,128]{1,0:T(8,128)S(1)} all-reduce(f32[40,128]{1,0:T(8,128)S(1)} %fusion.62), channel_id=1, replica_groups=mesh['rep'=8,'shard'=4] {'rep','shard'}, use_global_device_ids=true, to_apply=%region_10.11 | all-reduce | flops 5120 | bytes 40960 | tf_op jit(solution)/shard_map/psum | solution.py:309
  565.8 3.0 fusion.78
  568.8 14.3 %all-gather.15.cloned.1.call-done = bf16[768,3072]{1,0:T(8,128)(2,1)} async-done(((bf16[96,3072]{1,0:T(8,128)(2,1)}), bf16[768,3072]{1,0:T(8,128)(2,1)}) %all-gather.15.cloned.1.call-update) | async-done | bytes 4718608 | tf_op jit(solution)/shard_map/all_gather | solution.py:296
  583.1 7.4 %bitcast_convert_fusion.1 = f32[1,768,3072]{2,1,0:T(8,128)} fusion(bf16[768,3072]{1,0:T(8,128)(2,1)} %all-gather.15.cloned.1.call-done), kind=kLoop, calls=%fused_computation.15 | loop fusion | flops 2359296 | bytes 14155776 | tf_op jit(solution)/shard_map/broadcast_in_dim | solution.py:323
  590.5 33.6 %all-gather.17.cloned.1.call-done = bf16[3072,768]{1,0:T(8,128)(2,1)} async-done(((bf16[384,768]{1,0:T(8,128)(2,1)}), bf16[3072,768]{1,0:T(8,128)(2,1)}) %all-gather.17.cloned.1.call-update) | async-done | bytes 4718608 | tf_op jit(solution)/shard_map/all_gather | solution.py:295
  624.1 6.8 %bitcast_convert_fusion = f32[1,3072,768]{2,1,0:T(8,128)} fusion(bf16[3072,768]{1,0:T(8,128)(2,1)} %all-gather.17.cloned.1.call-done), kind=kLoop, calls=%fused_computation.14 | loop fusion | flops 2359296 | bytes 14155776 | tf_op jit(solution)/shard_map/broadcast_in_dim | solution.py:324
  (105 shorter events, 19.9 us)
Async XLA Ops:
  7.2 3.5 copy-start
  7.2 74.0 %copy-start.4 = (s32[1,256]{1,0:T(1,128)S(1)}, s32[1,256]{1,0:T(1,128)}, u32[]{:S(2)}) copy-start(s32[1,256]{1,0:T(1,128)} %row_ref.1) | copy-start | bytes 3076
  7.2 70.7 %all-gather.7.cloned.1.call-start = ((), (), s32[]{:S(2)}) async-start(), calls=%async_computation.5 | async-start | bytes 4866048 | tf_op jit(solution)/shard_map/all_gather | solution.py:171
  8.8 122.5 %all-gather.9.cloned.1.call-start = ((), (), s32[]{:S(2)}) async-start(), calls=%async_computation.6 | async-start | bytes 1966080 | tf_op jit(solution)/shard_map/all_gather | solution.py:222
  13.0 64.9 %copy-start.9 = (f32[256]{0:T(256)}, f32[256]{0:T(256)S(1)}, u32[]{:S(2)}) copy-start(f32[256]{0:T(256)S(1)} %add_rsqrt_fusion.1) | copy-start | bytes 3076
  13.0 79.4 %copy-start.5 = (bf16[256,768]{1,0:T(8,128)(2,1)S(1)}, bf16[256,768]{1,0:T(8,128)(2,1)}, u32[]{:S(2)}) copy-start(bf16[256,768]{1,0:T(8,128)(2,1)} %param.15) | copy-start | bytes 1179652
  81.2 13.1 %copy-start.7 = (f32[768]{0:T(1024)S(1)}, f32[768]{0:T(1024)}, u32[]{:S(2)}) copy-start(f32[768]{0:T(1024)} %param.21) | copy-start | bytes 9220
  81.2 14.8 %copy-start.16 = (s32[256,2]{0,1:T(2,128)S(1)}, s32[256,2]{0,1:T(2,128)}, u32[]{:S(2)}) copy-start(s32[256,2]{0,1:T(2,128)} %param.19) | copy-start | bytes 6148
  81.2 50.1 %copy-start.8 = (bf16[768,4]{0,1:T(4,128)(2,1)S(1)}, bf16[768,4]{0,1:T(4,128)(2,1)}, u32[]{:S(2)}) copy-start(bf16[768,4]{0,1:T(4,128)(2,1)} %param.27) | copy-start | bytes 18436
  90.8 1.7 copy-start.2
  94.3 147.3 %copy-start.12 = (f32[256]{0:T(256)}, f32[256]{0:T(256)S(1)}, u32[]{:S(2)}) copy-start(f32[256]{0:T(256)S(1)} %add_rsqrt_fusion) | copy-start | bytes 3076
  95.2 73.6 %all-gather.11.cloned.1.call-start = ((), (), s32[]{:S(2)}) async-start(), calls=%async_computation.8 | async-start | bytes 1966080 | tf_op jit(solution)/shard_map/all_gather | solution.py:205
  95.9 145.6 %reduce-scatter.8.cloned.1.call-start = ((), (), s32[]{:S(2)}) async-start(), calls=%async_computation.9 | async-start | bytes 1966080 | tf_op jit(solution)/shard_map/reduce_scatter | solution.py:260
  133.3 48.7 %copy-start.14 = (f32[1024,1]{0,1:T(1,128)}, f32[1024,1]{0,1:T(1,128)S(1)}, u32[]{:S(2)}) copy-start(f32[1024,1]{0,1:T(1,128)S(1)} %fusion.73) | copy-start | bytes 12292
  168.8 13.1 %copy-start.17 = (bf16[1024,768]{1,0:T(8,128)(2,1)S(1)}, bf16[1024,768]{1,0:T(8,128)(2,1)}, u32[]{:S(2)}) copy-start(bf16[1024,768]{1,0:T(8,128)(2,1)} %all-gather.11.cloned.1.call-done) | copy-start | bytes 4718596
  168.8 28.5 %slice-start = ((s8[4718592]{0:T(1024)(128)(4,1)}), s8[4194304]{0:T(1024)(128)(4,1)S(1)}, s32[]{:S(2)}) async-start(s8[4718592]{0:T(1024)(128)(4,1)} %bitcast.75), calls=%async_computation.16 | async-start | bytes 8388608
  182.0 15.3 %slice-start.1 = ((s8[4718592]{0:T(1024)(128)(4,1)}), s8[524288]{0:T(1024)(128)(4,1)S(1)}, s32[]{:S(2)}) async-start(s8[4718592]{0:T(1024)(128)(4,1)} %bitcast.75), calls=%async_computation.17 | async-start | bytes 1048576
  207.2 70.7 %reduce-scatter.6.cloned.1.call-start = ((), (), s32[]{:S(2)}) async-start(), calls=%async_computation.7 | async-start | bytes 1966080 | tf_op jit(solution)/shard_map/reduce_scatter | solution.py:268
  207.8 192.5 %reduce-scatter.10.cloned.1.call-start = ((), (), s32[]{:S(2)}) async-start(), calls=%async_computation.10 | async-start | bytes 4866048 | tf_op jit(solution)/shard_map/reduce_scatter | solution.py:175
  277.9 4.8 copy-start.3
  282.7 7.4 %copy-start.6 = (f32[768]{0:T(1024)S(1)}, f32[768]{0:T(1024)}, u32[]{:S(2)}) copy-start(f32[768]{0:T(1024)} %param.20) | copy-start | bytes 9220
  282.7 7.4 %copy-start.10 = (f32[256]{0:T(256)S(1)}, f32[256]{0:T(256)}, u32[]{:S(2)}) copy-start(f32[256]{0:T(256)} %copy-done.9) | copy-start | bytes 3076
  294.2 163.0 %reduce-scatter.12.cloned.1.call-start = ((), (), s32[]{:S(2)}) async-start(), calls=%async_computation.12 | async-start | bytes 5308416 | tf_op jit(solution)/shard_map/reduce_scatter | solution.py:267
  303.4 0.7 copy-start.15
  303.4 211.8 %reduce-scatter.14.cloned.1.call-start = ((), (), s32[]{:S(2)}) async-start(), calls=%async_computation.14 | async-start | bytes 5308416 | tf_op jit(solution)/shard_map/reduce_scatter | solution.py:266
  316.7 198.5 %copy-start.13 = (s32[383]{0:T(512)S(1)}, s32[383]{0:T(512)}, u32[]{:S(2)}) copy-start(s32[383]{0:T(512)} %param.18) | copy-start | bytes 4600
  316.7 249.1 %all-gather.13.cloned.1.call-start = ((), (), s32[]{:S(2)}) async-start(), calls=%async_computation.11 | async-start | bytes 1327104 | tf_op jit(solution)/shard_map/all_gather | solution.py:297
  400.4 182.7 %all-gather.15.cloned.1.call-start = ((), (), s32[]{:S(2)}) async-start(), calls=%async_computation.13 | async-start | bytes 5308416 | tf_op jit(solution)/shard_map/all_gather | solution.py:296
  457.3 166.8 %all-gather.17.cloned.1.call-start = ((), (), s32[]{:S(2)}) async-start(), calls=%async_computation.15 | async-start | bytes 5308416 | tf_op jit(solution)/shard_map/all_gather | solution.py:295
  518.4 3.9 copy-start.11
  583.1 47.8 %copy-start.1 = (f32[32,12]{0,1:T(8,128)S(1)}, f32[32,12]{0,1:T(8,128)}, u32[]{:S(2)}) copy-start(f32[32,12]{0,1:T(8,128)} %param.26) | copy-start | bytes 4612
Sparse Core Ops, SparseCore 0:
  11.5 66.3 all-gather.6
  95.3 35.9 all-gather.8
  132.9 35.9 all-gather.10
  207.3 34.1 reduce-scatter.7
  243.7 34.2 reduce-scatter.5
  294.4 105.9 reduce-scatter.9
  404.2 52.9 reduce-scatter.11
  461.2 53.8 reduce-scatter.13
  517.2 24.4 all-gather.12
  543.6 39.4 all-gather.14
  585.1 38.9 all-gather.16

commit v2 on v1

--- a/solution.py
+++ b/solution.py
@@ -166,13 +166,64 @@
     )(qkv, qkv, qkv, probs, grad_heads)
 
 
-def gather_projections(stacked, rep, piece):
-    part = lax.dynamic_slice_in_dim(stacked, rep * piece, piece, axis=0)
+def gather_projections(part):
     return lax.all_gather(part, ("shard", "rep"), axis=0, tiled=True)
 
 
+def turn(block, step):
+    count = lax.axis_size("shard")
+    return lax.ppermute(block, "shard", [(d, (d + step) % count) for d in range(count)])
+
+
+def swap(block, axis_name, bit):
+    count = lax.axis_size(axis_name)
+    return lax.ppermute(block, axis_name, [(d, d ^ bit) for d in range(count)])
+
+
+def spans(axis_name):
+    count = lax.axis_size(axis_name)
+    return [1 << b for b in range(count.bit_length() - 1)]
+
+
+def halve_sum(block, axis):
+    rep = lax.axis_index("rep")
+    for bit in spans("rep"):
+        upper = (rep // bit) % 2
+        half = block.shape[axis] // 2
+        kept = lax.dynamic_slice_in_dim(block, upper * half, half, axis)
+        sent = lax.dynamic_slice_in_dim(block, (1 - upper) * half, half, axis)
+        came = swap(sent, "rep", bit)
+        block = (kept.astype(jnp.float32) + came.astype(jnp.float32)).astype(LOW)
+    return block
+
+
+def double_up(block):
+    rep = lax.axis_index("rep")
+    for bit in reversed(spans("rep")):
+        upper = (rep // bit) % 2 == 1
+        came = swap(block, "rep", bit)
+        block = jnp.concatenate(
+            [jnp.where(upper, came, block), jnp.where(upper, block, came)], axis=0
+        )
+    return block
+
+
+def sum_everywhere(small):
+    for axis_name in ("rep", "shard"):
+        for bit in spans(axis_name):
+            small = small + swap(small, axis_name, bit)
+    return small
+
+
 def reduce_projections(whole):
-    return lax.psum_scatter(whole, ("shard", "rep"), scatter_dimension=0, tiled=True)
+    count = lax.axis_size("shard")
+    mine = lax.axis_index("shard")
+    held = halve_sum(whole.reshape(count, -1, whole.shape[1]), 1)
+    total = lax.dynamic_index_in_dim(held, mine, 0, keepdims=False).astype(jnp.float32)
+    for step in range(1, count):
+        block = lax.dynamic_index_in_dim(held, (mine + step) % count, 0, keepdims=False)
+        total = total + turn(block, step).astype(jnp.float32)
+    return total.astype(LOW)
 
 
 def on_device(
@@ -199,11 +250,16 @@
     width = 2 * rows_here
     inputs = tokens.astype(jnp.float32)
 
-    stacked = jnp.concatenate([w_query, w_key, w_value, w_proj], axis=1)
-    piece = stacked.shape[0] // reps
-    full = gather_projections(stacked, rep, piece)
-    all_cot = lax.all_gather(cotangent, "shard", axis=0, tiled=True)
-    all_routes = lax.all_gather(routes, "shard", axis=0, tiled=True)
+    shards = lax.axis_size("shard")
+    piece = w_query.shape[0] // reps
+    parts = [
+        lax.dynamic_slice_in_dim(w, rep * piece, piece, axis=0)
+        for w in (w_query, w_key, w_value, w_proj)
+    ]
+    full_qkv = gather_projections(jnp.concatenate(parts[:3], axis=1))
+    full_proj = gather_projections(parts[3])
+    cot_blocks = [cotangent] + [turn(cotangent, step) for step in range(1, shards)]
+    route_blocks = [routes] + [turn(routes, step) for step in range(1, shards)]
 
     onehot = gap_onehot(buckets, rel_table.shape[0], width)
     gaps = lax.dot_general(
@@ -211,63 +267,66 @@
     ).reshape(HEADS, 1, width)
     scale_first = inverse_rms(inputs)
     h_first = (inputs * scale_first * gain_attn).astype(LOW)
-    full_qkv = full[:, : 3 * model]
-    full_proj = full[:, 3 * model :]
     qkv = product(h_first, full_qkv).astype(LOW)
     probs, mixed_heads = attention(qkv, gaps, doc_ids[0])
     y_first = inputs + product(mixed_heads, full_proj)
     scale_second = inverse_rms(y_first)
     h_second = (y_first * scale_second * gain_moe).astype(LOW)
 
-    all_h = lax.all_gather(h_second, "shard", axis=0, tiled=True)
-    logits = product(all_h, w_router)
+    h_blocks = [h_second] + [turn(h_second, step) for step in range(1, shards)]
+    w_first, w_second = w_in[0], w_down[0]
     ids = jnp.arange(w_router.shape[1], dtype=jnp.int32)[None, :]
-    hot_first = (all_routes[:, 0:1] == ids).astype(jnp.float32)
-    hot_second = (all_routes[:, 1:2] == ids).astype(jnp.float32)
-    apart = hot_first - hot_second
-    gap_logit = jnp.sum(logits * apart, axis=1, keepdims=True)
-    gate_first = jax.nn.sigmoid(gap_logit)
-    gate_second = jax.nn.sigmoid(-gap_logit)
-    is_first = (all_routes[:, 0:1] == mine).astype(jnp.float32)
-    is_second = (all_routes[:, 1:2] == mine).astype(jnp.float32)
-    gate = is_first * gate_first + is_second * gate_second
-    out_grad_all = all_cot.astype(jnp.float32)
-    grad_eo = (out_grad_all * gate).astype(LOW)
-
-    w_first, w_second = w_in[0], w_down[0]
-    hidden = product(all_h, w_first)
-    act_full, gelu_pull = jax.vjp(jax.nn.gelu, hidden)
-    act_low = act_full.astype(LOW)
-    grad_act = inner_right(grad_eo, w_second)
-    grad_hidden = gelu_pull(grad_act)[0].astype(LOW)
-    expert_out = product(act_low, w_second).astype(LOW).astype(jnp.float32)
-    grad_rows = inner_right(grad_hidden, w_first)
-    grad_gate = jnp.sum(out_grad_all * expert_out, axis=1, keepdims=True)
-    grad_gap = grad_gate * (is_first - is_second) * gate_first * gate_second
-    grad_logits = grad_gap * apart
+    acts, grads_eo, grads_hidden, grads_logits = [], [], [], []
+    grad_h_second = jnp.zeros((rows_here, model), jnp.float32)
+    routed = jnp.zeros((rows_here, model), jnp.float32)
+    for step in range(shards):
+        h_here, route = h_blocks[step], route_blocks[step]
+        out_grad_here = cot_blocks[step].astype(jnp.float32)
+        logits = product(h_here, w_router)
+        apart = (route[:, 0:1] == ids).astype(jnp.float32) - (route[:, 1:2] == ids).astype(
+            jnp.float32
+        )
+        gap_logit = jnp.sum(logits * apart, axis=1, keepdims=True)
+        gate_first = jax.nn.sigmoid(gap_logit)
+        gate_second = jax.nn.sigmoid(-gap_logit)
+        is_first = (route[:, 0:1] == mine).astype(jnp.float32)
+        is_second = (route[:, 1:2] == mine).astype(jnp.float32)
+        gate = is_first * gate_first + is_second * gate_second
+        grad_eo = (out_grad_here * gate).astype(LOW)
+        act_full, gelu_pull = jax.vjp(jax.nn.gelu, product(h_here, w_first))
+        act_low = act_full.astype(LOW)
+        grad_hidden = gelu_pull(inner_right(grad_eo, w_second))[0].astype(LOW)
+        expert_out = product(act_low, w_second).astype(LOW).astype(jnp.float32)
+        grad_gate = jnp.sum(out_grad_here * expert_out, axis=1, keepdims=True)
+        grad_logits = grad_gate * (is_first - is_second) * gate_first * gate_second * apart
+        back_h = inner_right(grad_hidden, w_first) + lax.dot_general(
+            grad_logits,
+            w_router.astype(jnp.float32),
+            (((1,), (1,)), ((), ())),
+            precision=lax.Precision.HIGHEST,
+        )
+        out_here = gate * expert_out
+        if step:
+            back_h = turn(back_h.astype(LOW), shards - step).astype(jnp.float32)
+            out_here = turn(out_here.astype(LOW), shards - step).astype(jnp.float32)
+        grad_h_second = grad_h_second + back_h
+        routed = routed + out_here
+        acts.append(act_low)
+        grads_eo.append(grad_eo)
+        grads_hidden.append(grad_hidden)
+        grads_logits.append(grad_logits)
+    all_h = jnp.concatenate(h_blocks, axis=0)
+    grad_down = inner_left(jnp.concatenate(acts, axis=0), jnp.concatenate(grads_eo, axis=0))
+    grad_in = inner_left(all_h, jnp.concatenate(grads_hidden, axis=0))
+    part_in = lax.psum_scatter(grad_in.astype(LOW), "rep", scatter_dimension=0, tiled=True)
+    sum_in = lax.all_gather(part_in, "rep", axis=0, tiled=True).astype(jnp.float32)
+    part_down = halve_sum(grad_down.astype(LOW), 0)
     grad_router = lax.dot_general(
         all_h.astype(jnp.float32),
-        grad_logits,
+        jnp.concatenate(grads_logits, axis=0),
         (((0,), (0,)), ((), ())),
         precision=lax.Precision.HIGHEST,
     )
-    back_h = grad_rows + lax.dot_general(
-        grad_logits,
-        w_router.astype(jnp.float32),
-        (((1,), (1,)), ((), ())),
-        precision=lax.Precision.HIGHEST,
-    )
-    grad_h_second = lax.psum_scatter(
-        back_h.astype(LOW), "shard", scatter_dimension=0, tiled=True
-    ).astype(jnp.float32)
-
-    grad_down = inner_left(act_low, grad_eo).astype(LOW)
-    grad_in = inner_left(all_h, grad_hidden).astype(LOW)
-    part_down = lax.psum_scatter(grad_down, "rep", scatter_dimension=0, tiled=True)
-    part_in = lax.psum_scatter(grad_in, "rep", scatter_dimension=0, tiled=True)
-    routed = lax.psum_scatter(
-        (gate * expert_out).astype(LOW), "shard", scatter_dimension=0, tiled=True
-    ).astype(jnp.float32)
     mixed = (y_first + routed).astype(LOW)
 
     out_grad = cotangent.astype(jnp.float32)
@@ -292,9 +351,8 @@
     grad_x_part, grad_gain_attn = rms_pull(inputs, scale_first, gain_attn, grad_h_first)
     grad_tokens = grad_y_first + grad_x_part
 
-    sum_down = lax.all_gather(part_down, "rep", axis=0, tiled=True).astype(jnp.float32)
-    sum_in = lax.all_gather(part_in, "rep", axis=0, tiled=True).astype(jnp.float32)
-    own = lax.all_gather(own, "rep", axis=0, tiled=True).astype(jnp.float32)
+    sum_down = double_up(part_down).astype(jnp.float32)
+    own = double_up(own).astype(jnp.float32)
     small = jnp.concatenate(
         [
             grad_gain_attn,
@@ -306,7 +364,7 @@
     cut = small.shape[0]
     lines = -(-cut // 1024) * 8
     small = jnp.pad(small, (0, lines * 128 - cut)).reshape(lines, 128)
-    small = lax.psum(small, ("rep", "shard")).reshape(-1)
+    small = sum_everywhere(small).reshape(-1)
     marks = [model, 2 * model, 2 * model + w_router.size]
     sum_gain_attn, sum_gain_moe, sum_router, sum_table = jnp.split(small[:cut], marks)
     return (

time: 638 us -> 472 us (0.74); the launches traced: 637 us -> 464 us
  waiting for transfers between devices: 428 us -> 228 us
  starting transfers between devices: 0.92 us -> 60.4 us
  blocking collectives: 51.9 us -> 0 us
  local copies, waits for them, and re-layouts: 11.1 us -> 28.2 us
  other arithmetic: 26.8 us -> 39.3 us
  matrix products: 87.6 us -> 75.6 us
    reduce_scatter x5 -> x1, waiting for transfers between devices: 265 us -> 0.02 us  [on_device(): lax.psum_scatter(grad_in.astype(LOW), 'rep', scatter_dimension=0, tiled=T...]
    ppermute x0 -> x35, waiting for transfers between devices: none -> 152 us  [the longest x17 93.9 us: swap(): return lax.ppermute(block, axis_name, [(d, d ^ bit) for d in range(count)])]
    all_gather x4 -> x0, waiting for transfers between devices: 82.3 us -> none  [the longest x1 33.6 us: on_device(): lax.all_gather(part_down, 'rep', axis=0, tiled=True).astype(jnp.float32)]
    ppermute x0 -> x35, starting transfers between devices: none -> 60.3 us  [the longest x18 47 us: turn(): lax.ppermute(block, 'shard', [(d, (d + step) % count) for d in range(coun...]
    psum x1 -> x0, blocking collectives: 39.7 us -> none  [on_device(): small = lax.psum(small, ('rep', 'shard')).reshape(-1)]
    convert_element_type x0 -> x9, other arithmetic: none -> 14.8 us  [the longest x6 9.96 us: halve_sum(): block = (kept.astype(jnp.float32) + came.astype(jnp.float32)).astype(LOW)]
    all_gather x1, waiting for transfers between devices: 14.3 us -> 0.01 us  [on_device(): lax.all_gather(part_in, 'rep', axis=0, tiled=True).astype(jnp.float32)]
    all_gather x1 -> x0, blocking collectives: 12.2 us -> none  [on_device(): all_routes = lax.all_gather(routes, 'shard', axis=0, tiled=True)]
  transfers between devices with their start and end apart: 11 -> 39, of which waited for: 10 -> 17; matrix products, arithmetic and copies ran while one was open for 10% -> 26% of each run, Pallas kernels for 0% -> 4%
where the time goes in v2:
time: 472 us; the launch traced here: 464 us
  waiting for transfers between devices  228 us (48%)
  matrix products  75.6 us (16%)
  starting transfers between devices  60.4 us (13%)
  other arithmetic  39.3 us (8%)
  local copies, waits for them, and re-layouts  28.2 us (6%)
  Pallas kernels  17 us (4%)
  between operations  15.3 us (3%)
    ppermute x17, waiting for transfers between devices, swap(): return lax.ppermute(block, axis_name, [(d, d ^ bit) for d in range(count)])  93.9 us
    all_gather x2, waiting for transfers between devices, gather_projections(): return lax.all_gather(part, ('shard', 'rep'), axis=0, tiled=True)  75.9 us
    ppermute x18, waiting for transfers between devices, turn(): lax.ppermute(block, 'shard', [(d, (d + step) % count) for d in range(coun...  58.1 us
    ppermute x18, starting transfers between devices, turn(): lax.ppermute(block, 'shard', [(d, (d + step) % count) for d in range(coun...  47 us
    dot_general x14, matrix products, product(): return jnp.dot(left, right, preferred_element_type=jnp.float32)  29.7 us
    dot_general x10, matrix products, inner_right(): lax.dot_general(left, right, (((1,), (1,)), ((), ())), preferred_element_...  22.5 us
    dot_general x4, matrix products, inner_left(): lax.dot_general(left, right, (((0,), (0,)), ((), ())), preferred_element_...  15.1 us
    ppermute x17, starting transfers between devices, swap(): return lax.ppermute(block, axis_name, [(d, d ^ bit) for d in range(count)])  13.3 us
  transfers between devices with their start and end apart: 39, of which 17 were waited for; matrix products, arithmetic and copies ran while one was open for 26% of the time, Pallas kernels for 4%

profile of v2, /device:TPU:0, one launch (start us, length us, event | category | flops | bytes accessed | tf_op | source)
XLA Modules:
  0.0 463.7 jit_solution(5451397568184170055)
XLA Ops:
  11.1 5.1 %collective-permute-start.13 = (bf16[256,768]{1,0:T(8,128)(2,1)}, bf16[256,768]{1,0:T(8,128)(2,1)}, u32[]{:S(2)}, u32[]{:S(2)}) collective-permute-start(bf16[256,768]{1,0:T(8,128)(2,1)} %param.16), channel_id=1, source_target_pairs={{0,3},{1,0},{2,1},{3,2},{4,7},{5,4},{6,5},{7,6},{8,11},{9,8},{10,9... | collective-permute-start | bytes 1179656 | tf_op jit(solution)/shard_map/ppermute | solution.py:175
  27.7 8.1 %collective-permute-done.6 = s32[256,2]{0,1:T(2,128)S(1)} collective-permute-done((s32[256,2]{0,1:T(2,128)}, s32[256,2]{0,1:T(2,128)S(1)}, u32[]{:S(2)}, u32[]{:S(2)}) %collective-permute-start.6) | collective-permute-done | bytes 2080 | tf_op jit(solution)/shard_map/ppermute | solution.py:175
  35.8 17.3 %collective-permute-start = (s32[256,2]{0,1:T(2,128)}, s32[256,2]{0,1:T(2,128)S(1)}, u32[]{:S(2)}, u32[]{:S(2)}) collective-permute-start(s32[256,2]{0,1:T(2,128)} %param.19), channel_id=1, source_target_pairs={{0,1},{1,2},{2,3},{3,0},{4,5},{5,6},{6,7},{7,4},{8,9},{9,10},{10,1... | collective-permute-start | bytes 6152 | tf_op jit(solution)/shard_map/ppermute | solution.py:175
  54.6 34.0 %all-gather.4.cloned.1.call-done = bf16[768,2304]{1,0:T(8,128)(2,1)} async-done(((bf16[24,2304]{1,0:T(8,128)(2,1)}), bf16[768,2304]{1,0:T(8,128)(2,1)}) %all-gather.4.cloned.1.call-update) | async-done | bytes 3538960 | tf_op jit(solution)/shard_map/all_gather | solution.py:170
  88.7 3.3 convolution_convert_fusion.1.q_ref.k_ref.v_ref
  92.0 9.5 %shard_map.238 = (f32[12,256,256]{2,1,0:T(8,128)S(1)}, bf16[256,768]{1,0:T(8,128)(2,1)S(1)}) custom-call(bf16[256,2304]{1,0:T(8,128)(2,1)S(1)} %convolution_convert_fusion.1.q_ref.k_ref.v_ref, bf16[256,2304]{1,0:T(8,128)(2,1)S(1)} %convolution_convert_fusion.1.q_ref.k_ref.v_ref, bf16[256,2304]{1,0:T(8,128)(2,1)S(1)} %convolution_convert_fusion.1.q_ref.k_ref.v_ref, ...), custom_call_target="tpu_custom_call" | custom-call | flops 201326592 | bytes 3145728 | tf_op jit(solution)/shard_map/pallas_call | solution.py:85
  103.2 41.8 %all-gather.6.cloned.1.call-done = bf16[768,768]{1,0:T(8,128)(2,1)} async-done(((bf16[24,768]{1,0:T(8,128)(2,1)}), bf16[768,768]{1,0:T(8,128)(2,1)}) %all-gather.6.cloned.1.call-update) | async-done | bytes 1179664 | tf_op jit(solution)/shard_map/all_gather | solution.py:170
  149.4 4.4 multiply_convert_fusion.3
  165.0 3.5 fusion.137
  177.0 23.6 %collective-permute-done.4 = bf16[256,768]{1,0:T(8,128)(2,1)S(1)} collective-permute-done((bf16[256,768]{1,0:T(8,128)(2,1)S(1)}, bf16[256,768]{1,0:T(8,128)(2,1)S(1)}, u32[]{:S(2)}, u32[]{:S(2)}) %collective-permute-start.4) | collective-permute-done | bytes 393248 | tf_op jit(solution)/shard_map/ppermute | solution.py:175
  202.9 3.5 fusion.135
  206.4 3.3 fusion.74
  215.0 3.5 fusion.133
  218.5 2.9 fusion.67
  226.3 2.9 collective-permute-start.5
  229.3 6.8 %fusion.19 = bf16[768,3072]{1,0:T(8,128)(2,1)} fusion(bf16[256,3072]{1,0:T(8,128)(2,1)S(1)} %fusion.81, bf16[256,3072]{1,0:T(8,128)(2,1)S(1)} %fusion.74, bf16[256,3072]{1,0:T(8,128)(2,1)S(1)} %fusion.67, bf16[256,3072]{1,0:T(8,128)(2,1)S(1)} %fusion.60, bf16[256,768]{1,0:T(8,128)(2,1)S(1)} %collective-permute-done.7, ...), kind=kOutput, calls=%fused_computation.17 | convolution fusion | flops 4865654784 | bytes 12582912 | tf_op jit(solution)/shard_map/dot_general | solution.py:21
  241.5 4.3 collective-permute-done.8
  245.8 12.6 %collective-permute-done.5 = bf16[256,768]{1,0:T(8,128)(2,1)} collective-permute-done((bf16[256,768]{1,0:T(8,128)(2,1)}, bf16[256,768]{1,0:T(8,128)(2,1)}, u32[]{:S(2)}, u32[]{:S(2)}) %collective-permute-start.5) | collective-permute-done | bytes 393248 | tf_op jit(solution)/shard_map/ppermute | solution.py:175
  262.9 7.5 %shard_map.239 = (bf16[256,768]{1,0:T(8,128)(2,1)S(1)}, bf16[256,768]{1,0:T(8,128)(2,1)S(1)}, bf16[256,768]{1,0:T(8,128)(2,1)S(1)}, f32[12,1,512]{2,1,0:T(1,128)S(1)}) custom-call(bf16[256,2304]{1,0:T(8,128)(2,1)S(1)} %convolution_convert_fusion.1.q_ref.k_ref.v_ref, bf16[256,2304]{1,0:T(8,128)(2,1)S(1)} %convolution_convert_fusion.1.q_ref.k_ref.v_ref, ...), custom_call_target="tpu_custom_call" | custom-call | flops 402653184 | bytes 3145728 | tf_op jit(solution)/shard_map/pallas_call | solution.py:143
  275.0 6.5 %fusion.16 = bf16[3072,768]{1,0:T(8,128)(2,1)S(1)} fusion(bf16[256,3072]{1,0:T(8,128)(2,1)S(1)} %copy-done.40, bf16[256,3072]{1,0:T(8,128)(2,1)S(1)} %copy-done.42, bf16[256,3072]{1,0:T(8,128)(2,1)S(1)} %copy-done.44, bf16[256,3072]{1,0:T(8,128)(2,1)S(1)} %copy-done.38, bf16[256,768]{1,0:T(8,128)(2,1)S(1)} %copy-done.48, bf16[256,768]{1,0:T(8,128)(2,1)} %copy-done.49, ...), kind=kOutput, calls=%fused_computation.16 | convolution fusion | flops 4865654784 | bytes 12582912 | tf_op jit(solution)/shard_map/dot_general | solution.py:21
  291.7 4.0 fusion.143
  295.7 3.3 add_convert_fusion
  302.1 15.0 %collective-permute-done.21 = bf16[4,48,3072]{2,1,0:T(8,128)(2,1)} collective-permute-done((bf16[4,48,3072]{2,1,0:T(8,128)(2,1)}, bf16[4,48,3072]{2,1,0:T(8,128)(2,1)}, u32[]{:S(2)}, u32[]{:S(2)}) %collective-permute-start.21) | collective-permute-done | bytes 1179680 | tf_op jit(solution)/shard_map/ppermute | solution.py:180
  321.3 19.6 %collective-permute-done.30 = bf16[768,768]{1,0:T(8,128)(2,1)} collective-permute-done((bf16[768,768]{1,0:T(8,128)(2,1)}, bf16[768,768]{1,0:T(8,128)(2,1)}, u32[]{:S(2)}, u32[]{:S(2)}) %collective-permute-start.30) | collective-permute-done | bytes 1179680 | tf_op jit(solution)/shard_map/ppermute | solution.py:180
  345.0 6.4 %collective-permute-start.25 = (bf16[24,3072]{1,0:T(8,128)(2,1)S(1)}, bf16[24,3072]{1,0:T(8,128)(2,1)S(1)}, u32[]{:S(2)}, u32[]{:S(2)}) collective-permute-start(bf16[24,3072]{1,0:T(8,128)(2,1)S(1)} %get-tuple-element.64), channel_id=1, source_target_pairs={{0,3},{1,0},{2,1},{3,2},{4,7},{5,4},{6,5},{7,6},{8,11},{9,8},{10,9... | collective-permute-start | bytes 442376 | tf_op jit(solution)/shard_map/ppermute | solution.py:175
  352.7 4.7 %collective-permute-done.31 = bf16[384,768]{1,0:T(8,128)(2,1)} collective-permute-done((bf16[384,768]{1,0:T(8,128)(2,1)S(1)}, bf16[384,768]{1,0:T(8,128)(2,1)}, u32[]{:S(2)}, u32[]{:S(2)}) %collective-permute-start.31) | collective-permute-done | bytes 589856 | tf_op jit(solution)/shard_map/ppermute | solution.py:180
  359.0 5.4 %collective-permute-done.24 = bf16[24,3072]{1,0:T(8,128)(2,1)S(1)} collective-permute-done((bf16[24,3072]{1,0:T(8,128)(2,1)S(1)}, bf16[24,3072]{1,0:T(8,128)(2,1)S(1)}, u32[]{:S(2)}, u32[]{:S(2)}) %collective-permute-start.24) | collective-permute-done | bytes 147488 | tf_op jit(solution)/shard_map/ppermute | solution.py:175
  366.2 15.2 %collective-permute-done.32 = bf16[384,768]{1,0:T(8,128)(2,1)S(1)} collective-permute-done((bf16[384,768]{1,0:T(8,128)(2,1)S(1)}, bf16[384,768]{1,0:T(8,128)(2,1)S(1)}, u32[]{:S(2)}, u32[]{:S(2)}) %collective-permute-start.32) | collective-permute-done | bytes 589856 | tf_op jit(solution)/shard_map/ppermute | solution.py:180
  383.3 3.2 collective-permute-done.26
  388.7 32.6 %collective-permute-done.16 = f32[40,128]{1,0:T(8,128)S(1)} collective-permute-done((f32[40,128]{1,0:T(8,128)S(1)}, f32[40,128]{1,0:T(8,128)S(1)}, u32[]{:S(2)}, u32[]{:S(2)}) %collective-permute-start.16) | collective-permute-done | bytes 20512 | tf_op jit(solution)/shard_map/ppermute | solution.py:180
  445.0 4.5 maximum_convert_fusion
  449.5 7.4 %bitcast_convert_fusion = f32[1,768,3072]{2,1,0:T(8,128)} fusion(bf16[768,3072]{1,0:T(8,128)(2,1)} %all-gather.8.cloned.1.call-done), kind=kLoop, calls=%fused_computation.21 | loop fusion | flops 2359296 | bytes 14155776 | tf_op jit(solution)/shard_map/broadcast_in_dim | solution.py:381
  (290 shorter events, 122.7 us)
Async XLA Ops:
  7.2 81.5 %all-gather.4.cloned.1.call-start = ((), (), s32[]{:S(2)}) async-start(), calls=%async_computation.1 | async-start | bytes 3649536 | tf_op jit(solution)/shard_map/all_gather | solution.py:170
  9.6 135.4 %all-gather.6.cloned.1.call-start = ((), (), s32[]{:S(2)}) async-start(), calls=%async_computation.2 | async-start | bytes 1216512 | tf_op jit(solution)/shard_map/all_gather | solution.py:170
  11.1 333.8 %reduce-scatter.2.cloned.1.call-start = ((), (), s32[]{:S(2)}) async-start(), calls=%async_computation.3 | async-start | bytes 5308416 | tf_op jit(solution)/shard_map/reduce_scatter | solution.py:321
  11.1 153.8 %collective-permute-start.13 = (bf16[256,768]{1,0:T(8,128)(2,1)}, bf16[256,768]{1,0:T(8,128)(2,1)}, u32[]{:S(2)}, u32[]{:S(2)}) collective-permute-start(bf16[256,768]{1,0:T(8,128)(2,1)} %param.16), channel_id=1, source_target_pairs={{0,3},{1,0},{2,1},{3,2},{4,7},{5,4},{6,5},{7,6},{8,11},{9,8},{10,9... | collective-permute-start | bytes 1179656 | tf_op jit(solution)/shard_map/ppermute | solution.py:175
  16.2 186.7 %collective-permute-start.11 = (bf16[256,768]{1,0:T(8,128)(2,1)}, bf16[256,768]{1,0:T(8,128)(2,1)}, u32[]{:S(2)}, u32[]{:S(2)}) collective-permute-start(bf16[256,768]{1,0:T(8,128)(2,1)} %param.16), channel_id=1, source_target_pairs={{0,2},{1,3},{2,0},{3,1},{4,6},{5,7},{6,4},{7,5},{8,10},{9,11},{10,... | collective-permute-start | bytes 1179656 | tf_op jit(solution)/shard_map/ppermute | solution.py:175
  16.2 19.6 %collective-permute-start.6 = (s32[256,2]{0,1:T(2,128)}, s32[256,2]{0,1:T(2,128)S(1)}, u32[]{:S(2)}, u32[]{:S(2)}) collective-permute-start(s32[256,2]{0,1:T(2,128)} %param.19), channel_id=1, source_target_pairs={{0,3},{1,0},{2,1},{3,2},{4,7},{5,4},{6,5},{7,6},{8,11},{9,8},{10,9... | collective-permute-start | bytes 6152 | tf_op jit(solution)/shard_map/ppermute | solution.py:175
  16.7 36.4 %collective-permute-start.3 = (s32[256,2]{0,1:T(2,128)}, s32[256,2]{0,1:T(2,128)S(1)}, u32[]{:S(2)}, u32[]{:S(2)}) collective-permute-start(s32[256,2]{0,1:T(2,128)} %param.19), channel_id=1, source_target_pairs={{0,2},{1,3},{2,0},{3,1},{4,6},{5,7},{6,4},{7,5},{8,10},{9,11},{10,... | collective-permute-start | bytes 6152 | tf_op jit(solution)/shard_map/ppermute | solution.py:175
  19.2 195.8 %collective-permute-start.9 = (bf16[256,768]{1,0:T(8,128)(2,1)}, bf16[256,768]{1,0:T(8,128)(2,1)}, u32[]{:S(2)}, u32[]{:S(2)}) collective-permute-start(bf16[256,768]{1,0:T(8,128)(2,1)} %param.16), channel_id=1, source_target_pairs={{0,1},{1,2},{2,3},{3,0},{4,5},{5,6},{6,7},{7,4},{8,9},{9,10},{10,1... | collective-permute-start | bytes 1179656 | tf_op jit(solution)/shard_map/ppermute | solution.py:175
  35.8 18.8 %collective-permute-start = (s32[256,2]{0,1:T(2,128)}, s32[256,2]{0,1:T(2,128)S(1)}, u32[]{:S(2)}, u32[]{:S(2)}) collective-permute-start(s32[256,2]{0,1:T(2,128)} %param.19), channel_id=1, source_target_pairs={{0,1},{1,2},{2,3},{3,0},{4,5},{5,6},{6,7},{7,4},{8,9},{9,10},{10,1... | collective-permute-start | bytes 6152 | tf_op jit(solution)/shard_map/ppermute | solution.py:175
  147.1 14.5 %collective-permute-start.7 = (bf16[256,768]{1,0:T(8,128)(2,1)S(1)}, bf16[256,768]{1,0:T(8,128)(2,1)S(1)}, u32[]{:S(2)}, u32[]{:S(2)}) collective-permute-start(bf16[256,768]{1,0:T(8,128)(2,1)S(1)} %multiply_convert_fusion.7), channel_id=1, source_target_pairs={{0,3},{1,0},{2,1},{3,2},{4,7},{5,4},{6,5},{7,6},{8,11},{9,8},{10,9... | collective-permute-start | bytes 1179656 | tf_op jit(solution)/shard_map/ppermute | solution.py:175
  149.4 51.1 %collective-permute-start.4 = (bf16[256,768]{1,0:T(8,128)(2,1)S(1)}, bf16[256,768]{1,0:T(8,128)(2,1)S(1)}, u32[]{:S(2)}, u32[]{:S(2)}) collective-permute-start(bf16[256,768]{1,0:T(8,128)(2,1)S(1)} %multiply_convert_fusion.7), channel_id=1, source_target_pairs={{0,2},{1,3},{2,0},{3,1},{4,6},{5,7},{6,4},{7,5},{8,10},{9,11},{10,... | collective-permute-start | bytes 1179656 | tf_op jit(solution)/shard_map/ppermute | solution.py:175
  161.6 51.0 %collective-permute-start.1 = (bf16[256,768]{1,0:T(8,128)(2,1)S(1)}, bf16[256,768]{1,0:T(8,128)(2,1)S(1)}, u32[]{:S(2)}, u32[]{:S(2)}) collective-permute-start(bf16[256,768]{1,0:T(8,128)(2,1)S(1)} %multiply_convert_fusion.7), channel_id=1, source_target_pairs={{0,1},{1,2},{2,3},{3,0},{4,5},{5,6},{6,7},{7,4},{8,9},{9,10},{10,1... | collective-permute-start | bytes 1179656 | tf_op jit(solution)/shard_map/ppermute | solution.py:175
  174.2 62.0 %collective-permute-start.14 = (bf16[256,768]{1,0:T(8,128)(2,1)}, bf16[256,768]{1,0:T(8,128)(2,1)}, u32[]{:S(2)}, u32[]{:S(2)}) collective-permute-start(bf16[256,768]{1,0:T(8,128)(2,1)} %fusion.99), channel_id=1, source_target_pairs={{0,1},{1,2},{2,3},{3,0},{4,5},{5,6},{6,7},{7,4},{8,9},{9,10},{10,1... | collective-permute-start | bytes 1179656 | tf_op jit(solution)/shard_map/ppermute | solution.py:175
  212.6 24.6 %collective-permute-start.12 = (bf16[256,768]{1,0:T(8,128)(2,1)}, bf16[256,768]{1,0:T(8,128)(2,1)}, u32[]{:S(2)}, u32[]{:S(2)}) collective-permute-start(bf16[256,768]{1,0:T(8,128)(2,1)} %fusion.98), channel_id=1, source_target_pairs={{0,2},{1,3},{2,0},{3,1},{4,6},{5,7},{6,4},{7,5},{8,10},{9,11},{10,... | collective-permute-start | bytes 1179656 | tf_op jit(solution)/shard_map/ppermute | solution.py:175
  224.3 15.4 %collective-permute-start.10 = (bf16[256,768]{1,0:T(8,128)(2,1)}, bf16[256,768]{1,0:T(8,128)(2,1)}, u32[]{:S(2)}, u32[]{:S(2)}) collective-permute-start(bf16[256,768]{1,0:T(8,128)(2,1)} %fusion.97), channel_id=1, source_target_pairs={{0,3},{1,0},{2,1},{3,2},{4,7},{5,4},{6,5},{7,6},{8,11},{9,8},{10,9... | collective-permute-start | bytes 1179656 | tf_op jit(solution)/shard_map/ppermute | solution.py:175
  224.3 21.5 %collective-permute-start.8 = (bf16[256,768]{1,0:T(8,128)(2,1)}, bf16[256,768]{1,0:T(8,128)(2,1)}, u32[]{:S(2)}, u32[]{:S(2)}) collective-permute-start(bf16[256,768]{1,0:T(8,128)(2,1)} %get-tuple-element.60), channel_id=1, source_target_pairs={{0,1},{1,2},{2,3},{3,0},{4,5},{5,6},{6,7},{7,4},{8,9},{9,10},{10,1... | collective-permute-start | bytes 1179656 | tf_op jit(solution)/shard_map/ppermute | solution.py:175
  226.3 32.1 %collective-permute-start.5 = (bf16[256,768]{1,0:T(8,128)(2,1)}, bf16[256,768]{1,0:T(8,128)(2,1)}, u32[]{:S(2)}, u32[]{:S(2)}) collective-permute-start(bf16[256,768]{1,0:T(8,128)(2,1)} %get-tuple-element.58), channel_id=1, source_target_pairs={{0,2},{1,3},{2,0},{3,1},{4,6},{5,7},{6,4},{7,5},{8,10},{9,11},{10,... | collective-permute-start | bytes 1179656 | tf_op jit(solution)/shard_map/ppermute | solution.py:175
  236.1 213.4 %all-gather.8.cloned.1.call-start = ((), (), s32[]{:S(2)}) async-start(), calls=%async_computation.4 | async-start | bytes 5308416 | tf_op jit(solution)/shard_map/all_gather | solution.py:322
  236.2 22.2 %collective-permute-start.2 = (bf16[256,768]{1,0:T(8,128)(2,1)}, bf16[256,768]{1,0:T(8,128)(2,1)S(1)}, u32[]{:S(2)}, u32[]{:S(2)}) collective-permute-start(bf16[256,768]{1,0:T(8,128)(2,1)} %get-tuple-element.56), channel_id=1, source_target_pairs={{0,3},{1,0},{2,1},{3,2},{4,7},{5,4},{6,5},{7,6},{8,11},{9,8},{10,9... | collective-permute-start | bytes 1179656 | tf_op jit(solution)/shard_map/ppermute | solution.py:175
  283.3 12.4 %collective-permute-start.29 = (bf16[1536,768]{1,0:T(8,128)(2,1)}, bf16[1536,768]{1,0:T(8,128)(2,1)}, u32[]{:S(2)}, u32[]{:S(2)}) collective-permute-start(bf16[1536,768]{1,0:T(8,128)(2,1)} %constant_dynamic-slice_fusion.2), channel_id=1, source_target_pairs={{0,4},{4,0},{8,12},{12,8},{16,20},{20,16},{24,28},{28,24},{1,5},{5... | collective-permute-start | bytes 7077896 | tf_op jit(solution)/shard_map/ppermute | solution.py:180
  287.9 29.2 %collective-permute-start.21 = (bf16[4,48,3072]{2,1,0:T(8,128)(2,1)}, bf16[4,48,3072]{2,1,0:T(8,128)(2,1)}, u32[]{:S(2)}, u32[]{:S(2)}) collective-permute-start(bf16[4,48,3072]{2,1,0:T(8,128)(2,1)} %constant_dynamic-slice_fusion.4), channel_id=1, source_target_pairs={{0,8},{4,12},{8,0},{12,4},{16,24},{20,28},{24,16},{28,20},{1,9},{5... | collective-permute-start | bytes 3538952 | tf_op jit(solution)/shard_map/ppermute | solution.py:180
  300.1 40.7 %collective-permute-start.30 = (bf16[768,768]{1,0:T(8,128)(2,1)}, bf16[768,768]{1,0:T(8,128)(2,1)}, u32[]{:S(2)}, u32[]{:S(2)}) collective-permute-start(bf16[768,768]{1,0:T(8,128)(2,1)} %constant_dynamic-slice_fusion.1), channel_id=1, source_target_pairs={{0,8},{4,12},{8,0},{12,4},{16,24},{20,28},{24,16},{28,20},{1,9},{5... | collective-permute-start | bytes 3538952 | tf_op jit(solution)/shard_map/ppermute | solution.py:180
  320.7 22.9 %collective-permute-start.22 = (bf16[4,24,3072]{2,1,0:T(8,128)(2,1)}, bf16[4,24,3072]{2,1,0:T(8,128)(2,1)}, u32[]{:S(2)}, u32[]{:S(2)}) collective-permute-start(bf16[4,24,3072]{2,1,0:T(8,128)(2,1)} %constant_dynamic-slice_fusion.3), channel_id=1, source_target_pairs={{0,16},{4,20},{8,24},{12,28},{16,0},{20,4},{24,8},{28,12},{1,17},{... | collective-permute-start | bytes 1769480 | tf_op jit(solution)/shard_map/ppermute | solution.py:180
  321.2 66.0 %collective-permute-start.15 = (f32[40,128]{1,0:T(8,128)S(1)}, f32[40,128]{1,0:T(8,128)S(1)}, u32[]{:S(2)}, u32[]{:S(2)}) collective-permute-start(f32[40,128]{1,0:T(8,128)S(1)} %fusion.162), channel_id=1, source_target_pairs={{0,4},{4,0},{8,12},{12,8},{16,20},{20,16},{24,28},{28,24},{1,5},{5... | collective-permute-start | bytes 61448 | tf_op jit(solution)/shard_map/ppermute | solution.py:180
  343.5 13.9 %collective-permute-start.31 = (bf16[384,768]{1,0:T(8,128)(2,1)S(1)}, bf16[384,768]{1,0:T(8,128)(2,1)}, u32[]{:S(2)}, u32[]{:S(2)}) collective-permute-start(bf16[384,768]{1,0:T(8,128)(2,1)S(1)} %constant_dynamic-slice_fusion), channel_id=1, source_target_pairs={{0,16},{4,20},{8,24},{12,28},{16,0},{20,4},{24,8},{28,12},{1,17},{... | collective-permute-start | bytes 1769480 | tf_op jit(solution)/shard_map/ppermute | solution.py:180
  345.0 14.0 %collective-permute-start.25 = (bf16[24,3072]{1,0:T(8,128)(2,1)S(1)}, bf16[24,3072]{1,0:T(8,128)(2,1)S(1)}, u32[]{:S(2)}, u32[]{:S(2)}) collective-permute-start(bf16[24,3072]{1,0:T(8,128)(2,1)S(1)} %get-tuple-element.64), channel_id=1, source_target_pairs={{0,3},{1,0},{2,1},{3,2},{4,7},{5,4},{6,5},{7,6},{8,11},{9,8},{10,9... | collective-permute-start | bytes 442376 | tf_op jit(solution)/shard_map/ppermute | solution.py:175
  351.3 13.1 %collective-permute-start.24 = (bf16[24,3072]{1,0:T(8,128)(2,1)S(1)}, bf16[24,3072]{1,0:T(8,128)(2,1)S(1)}, u32[]{:S(2)}, u32[]{:S(2)}) collective-permute-start(bf16[24,3072]{1,0:T(8,128)(2,1)S(1)} %get-tuple-element.65), channel_id=1, source_target_pairs={{0,2},{1,3},{2,0},{3,1},{4,6},{5,7},{6,4},{7,5},{8,10},{9,11},{10,... | collective-permute-start | bytes 442376 | tf_op jit(solution)/shard_map/ppermute | solution.py:175
  358.6 22.8 %collective-permute-start.32 = (bf16[384,768]{1,0:T(8,128)(2,1)S(1)}, bf16[384,768]{1,0:T(8,128)(2,1)S(1)}, u32[]{:S(2)}, u32[]{:S(2)}) collective-permute-start(bf16[384,768]{1,0:T(8,128)(2,1)S(1)} %add_convert_fusion.4), channel_id=1, source_target_pairs={{0,16},{4,20},{8,24},{12,28},{16,0},{20,4},{24,8},{28,12},{1,17},{... | collective-permute-start | bytes 1769480 | tf_op jit(solution)/shard_map/ppermute | solution.py:180
  364.5 22.0 %collective-permute-start.26 = (bf16[24,3072]{1,0:T(8,128)(2,1)S(1)}, bf16[24,3072]{1,0:T(8,128)(2,1)S(1)}, u32[]{:S(2)}, u32[]{:S(2)}) collective-permute-start(bf16[24,3072]{1,0:T(8,128)(2,1)S(1)} %fusion.149), channel_id=1, source_target_pairs={{0,16},{4,20},{8,24},{12,28},{16,0},{20,4},{24,8},{28,12},{1,17},{... | collective-permute-start | bytes 442376 | tf_op jit(solution)/shard_map/ppermute | solution.py:180
  382.5 44.3 %collective-permute-start.33 = (bf16[768,768]{1,0:T(8,128)(2,1)S(1)}, bf16[768,768]{1,0:T(8,128)(2,1)}, u32[]{:S(2)}, u32[]{:S(2)}) collective-permute-start(bf16[768,768]{1,0:T(8,128)(2,1)S(1)} %pad_maximum_fusion.3), channel_id=1, source_target_pairs={{0,8},{4,12},{8,0},{12,4},{16,24},{20,28},{24,16},{28,20},{1,9},{5... | collective-permute-start | bytes 3538952 | tf_op jit(solution)/shard_map/ppermute | solution.py:180
  386.6 40.1 %collective-permute-start.27 = (bf16[48,3072]{1,0:T(8,128)(2,1)S(1)}, bf16[48,3072]{1,0:T(8,128)(2,1)S(1)}, u32[]{:S(2)}, u32[]{:S(2)}) collective-permute-start(bf16[48,3072]{1,0:T(8,128)(2,1)S(1)} %pad_maximum_fusion.5), channel_id=1, source_target_pairs={{0,8},{4,12},{8,0},{12,4},{16,24},{20,28},{24,16},{28,20},{1,9},{5... | collective-permute-start | bytes 884744 | tf_op jit(solution)/shard_map/ppermute | solution.py:180
  387.2 34.1 %collective-permute-start.16 = (f32[40,128]{1,0:T(8,128)S(1)}, f32[40,128]{1,0:T(8,128)S(1)}, u32[]{:S(2)}, u32[]{:S(2)}) collective-permute-start(f32[40,128]{1,0:T(8,128)S(1)} %fusion.244), channel_id=1, source_target_pairs={{0,8},{4,12},{8,0},{12,4},{16,24},{20,28},{24,16},{28,20},{1,9},{5... | collective-permute-start | bytes 61448 | tf_op jit(solution)/shard_map/ppermute | solution.py:180
  (62 other events, 667.0 us)
Sparse Core Ops, SparseCore 0:
  11.5 77.1 all-gather.3
  92.1 52.8 all-gather.5
  236.2 50.5 reduce-scatter.1
  345.0 52.9 all-gather.7
